TPU v7x, 512 devices: a whole 4x4x16 slice. The times are simulated.
512 devices in a mesh: peer: 32 (over y_lo, z), grp: 16 (over y_hi, x, core).
Axes of the slice: x: 4, y: 4 (y_hi: 2, y_lo: 2; y = y_hi * 2 + y_lo), z: 16, core: 2. Of those that a mesh axis runs over, the one named last changes fastest.
Arguments:
- tokens: bfloat16 [65536, 2048], P(('peer', 'grp')), may hold values from -6 to 6
- cotangent: bfloat16 [65536, 2048], P(('peer', 'grp')), may hold values from -6 to 6
- expert_ids: int32 [65536, 4], P(('peer', 'grp')), may hold values from 0 to 31, all different within a row; in each aligned block of 128 rows (0 to 127, 128 to 255, ...) at most 32 rows name the same one
- route_prob: float32 [65536, 4], P(('peer', 'grp')), may hold values from 0.1 to 1
- w_gate: bfloat16 [32, 2048, 2816], P('peer', None, 'grp'), may hold values from -0.125 to 0.125
- w_up: bfloat16 [32, 2048, 2816], P('peer', None, 'grp'), may hold values from -0.125 to 0.125
- w_down: bfloat16 [32, 2816, 2048], P('peer', 'grp'), may hold values from -0.21875 to 0.21875
- student_logits: bfloat16 [32, 8, 151936], P('peer', None, 'grp'), may hold values from -24 to 252
- stale_logits: bfloat16 [32, 8, 151936], P('peer', None, 'grp'), may hold values from -24 to 252
- labels: int32 [32, 8], P('peer'), may hold values from 0 to 151935
Outputs:
- layer_out: bfloat16 [65536, 2048], P(('peer', 'grp'))
- input_grad: bfloat16 [65536, 2048], P(('peer', 'grp'))
- prob_grad: float32 [65536, 4], P(('peer', 'grp'))
- distill_loss: float32 [32, 8], P('peer')
- logit_grad: bfloat16 [32, 8, 151936], P('peer', None, 'grp')
Inputs may be any that keep to these rules, and one draw needn't show every extreme that they name: `expert_ids`: each row names 4 different experts; the rows of one device name any one expert at most 32 times.
All inputs are finite; a program needn't handle non-finite values.
Results may differ from a plain program's by a relative error of at most 0.0064.
Values may be sent and summed in bfloat16 or wider, within the bound.
A program may use at most 64 MiB of HBM per device.

v0:
```python
import jax
import jax.numpy as jnp
from jax import lax
from jax.sharding import PartitionSpec as P

PIECES = 4
CAP = 32


def from_behind(value, axis, steps):
    count = lax.axis_size(axis)
    pairs = [(source, (source + steps) % count) for source in range(count)]
    return lax.ppermute(value, axis, pairs)


def slot_tables(expert_ids, n_window, capacity):
    window_iota = lax.broadcasted_iota(jnp.int32, (1, 1, n_window), 2)
    member = jnp.sum((expert_ids[:, :, None] == window_iota).astype(jnp.int32), axis=1)
    position = jnp.cumsum(member, axis=0) - member
    slot_iota = lax.broadcasted_iota(jnp.int32, (1, capacity, 1), 1)
    select = (position.T[:, None, :] == slot_iota) & (member.T[:, None, :] > 0)
    return (position, select)


def forward_piece(slot_rows, gate_cols, up_cols, down_rows):
    gate_act = jnp.dot(slot_rows, gate_cols, preferred_element_type=jnp.float32)
    up_act = jnp.dot(slot_rows, up_cols, preferred_element_type=jnp.float32)
    hidden = (gate_act * jax.nn.sigmoid(gate_act) * up_act).astype(jnp.bfloat16)
    piece_out = jnp.dot(hidden, down_rows, preferred_element_type=jnp.float32).astype(jnp.bfloat16)
    return (piece_out, gate_act, up_act)


def backward_piece(scaled_rows, gate_act, up_act, gate_cols, up_cols, down_rows):
    contract = (((1,), (1,)), ((), ()))
    grad_hidden = lax.dot_general(
        scaled_rows, down_rows, contract, preferred_element_type=jnp.float32
    )
    sigmoid_gate = jax.nn.sigmoid(gate_act)
    grad_gate = (
        grad_hidden * up_act * sigmoid_gate * (1.0 + gate_act * (1.0 - sigmoid_gate))
    ).astype(jnp.bfloat16)
    grad_up = (grad_hidden * gate_act * sigmoid_gate).astype(jnp.bfloat16)
    piece_grad = lax.dot_general(grad_gate, gate_cols, contract, preferred_element_type=jnp.float32)
    piece_grad = piece_grad + lax.dot_general(
        grad_up, up_cols, contract, preferred_element_type=jnp.float32
    )
    return piece_grad.astype(jnp.bfloat16)


def distill(student_logits, teacher_now, labels):
    student = student_logits[0].astype(jnp.float32)
    teacher = teacher_now[0].astype(jnp.float32)
    shard_width = student.shape[1]
    vocab_ids = lax.axis_index("grp") * shard_width + lax.broadcasted_iota(
        jnp.int32, student.shape, 1
    )
    label_hit = vocab_ids == labels[0][:, None]
    label_logit = jnp.sum(jnp.where(label_hit, student, 0.0), axis=1)
    local_smax = jnp.max(student, axis=1)
    local_tmax = jnp.max(teacher, axis=1)
    max_student, max_teacher = lax.pmax((local_smax, local_tmax), "grp")
    student_exp = jnp.sum(jnp.exp(student - max_student[:, None]), axis=1)
    teacher_exp = jnp.exp(teacher - max_teacher[:, None])
    teacher_sum = jnp.sum(teacher_exp, axis=1)
    cross_sum = jnp.sum(teacher_exp * (teacher - student), axis=1)
    student_sum, teacher_sum, cross_sum, label_logit = lax.psum(
        (student_exp, teacher_sum, cross_sum, label_logit), "grp"
    )
    lse_student = max_student + jnp.log(student_sum)
    lse_teacher = max_teacher + jnp.log(teacher_sum)
    distill_loss = 2.0 * lse_student - label_logit + cross_sum / teacher_sum - lse_teacher
    teacher_prob = jnp.exp(teacher - lse_teacher[:, None])
    logit_grad = (
        2.0 * jnp.exp(student - lse_student[:, None]) - label_hit.astype(jnp.float32) - teacher_prob
    ).astype(jnp.bfloat16)
    return (distill_loss[None], logit_grad[None])


def body(
    tokens,
    cotangent,
    expert_ids,
    route_prob,
    w_gate,
    w_up,
    w_down,
    student_logits,
    stale_logits,
    labels,
):
    group_size = lax.axis_size("grp")
    n_window = group_size // PIECES
    gate_cols = w_gate[0]
    up_cols = w_up[0]
    down_rows = w_down[0]
    model_width = tokens.shape[1]
    half_cap = CAP // 2
    position, select = slot_tables(expert_ids, n_window, CAP)
    select_bf = select.astype(jnp.bfloat16)
    window_iota = lax.broadcasted_iota(jnp.int32, (1, 1, n_window), 2)
    token_prob = jnp.sum(
        route_prob[:, :, None] * (expert_ids[:, :, None] == window_iota).astype(jnp.float32), axis=1
    )
    slot_prob = jnp.einsum(
        "ect,te->ec", select.astype(jnp.float32), token_prob, precision=lax.Precision.HIGHEST
    )
    slot_rows = jnp.einsum(
        "ect,td->ecd", select_bf, tokens, preferred_element_type=jnp.float32
    ).astype(jnp.bfloat16)
    slot_cot = jnp.einsum("ect,td->ecd", select_bf, cotangent, preferred_element_type=jnp.float32)
    slot_scaled = (slot_prob[:, :, None] * slot_cot).astype(jnp.bfloat16)
    send_rows = jnp.repeat(slot_rows, PIECES, axis=0).reshape(group_size, 2, half_cap, model_width)
    send_scaled = jnp.repeat(slot_scaled, PIECES, axis=0).reshape(
        group_size, 2, half_cap, model_width
    )
    recv_rows = lax.all_to_all(send_rows, "grp", split_axis=0, concat_axis=0, tiled=True)
    recv_scaled = lax.all_to_all(send_scaled, "grp", split_axis=0, concat_axis=0, tiled=True)
    item_count = recv_rows.shape[1]
    flat_rows = recv_rows.reshape(-1, model_width)
    flat_scaled = recv_scaled.reshape(-1, model_width)
    piece_out, gate_act, up_act = forward_piece(flat_rows, gate_cols, up_cols, down_rows)
    piece_out = piece_out.reshape(group_size, item_count, half_cap, model_width)
    piece_grad = backward_piece(flat_scaled, gate_act, up_act, gate_cols, up_cols, down_rows)
    piece_grad = piece_grad.reshape(group_size, item_count, half_cap, model_width)
    back_out = lax.all_to_all(piece_out, "grp", split_axis=0, concat_axis=0, tiled=True)
    back_grad = lax.all_to_all(piece_grad, "grp", split_axis=0, concat_axis=0, tiled=True)
    back_out, back_grad = (back_out, back_grad)
    expert_out = jnp.sum(
        back_out.astype(jnp.float32).reshape(n_window, PIECES, CAP, model_width), axis=1
    )
    expert_grad = jnp.sum(
        back_grad.astype(jnp.float32).reshape(n_window, PIECES, CAP, model_width), axis=1
    )
    in_window = expert_ids < n_window
    safe_ids = jnp.where(in_window, expert_ids, 0)
    slot_index = jnp.take_along_axis(position, safe_ids, axis=1)
    flat_index = safe_ids * CAP + slot_index
    out_rows = jnp.where(
        in_window[:, :, None],
        jnp.take(expert_out.reshape(-1, model_width), flat_index, axis=0),
        0.0,
    )
    grad_rows = jnp.where(
        in_window[:, :, None],
        jnp.take(expert_grad.reshape(-1, model_width), flat_index, axis=0),
        0.0,
    )
    layer_out = jnp.sum(route_prob[:, :, None] * out_rows, axis=1).astype(jnp.bfloat16)
    prob_grad = jnp.sum(cotangent.astype(jnp.float32)[:, None, :] * out_rows, axis=2)
    input_grad = jnp.sum(grad_rows, axis=1).astype(jnp.bfloat16)
    teacher_now = from_behind(stale_logits, "peer", 1)
    distill_loss, logit_grad = distill(student_logits, teacher_now, labels)
    return (layer_out, input_grad, prob_grad, distill_loss, logit_grad)


def solution(mesh):
    placed = (
        P(("peer", "grp"), None),
        P(("peer", "grp"), None),
        P(("peer", "grp"), None),
        P(("peer", "grp"), None),
        P("peer", None, "grp"),
        P("peer", None, "grp"),
        P("peer", "grp", None),
        P("peer", None, "grp"),
        P("peer", None, "grp"),
        P("peer", None),
    )
    return jax.shard_map(
        body,
        mesh=mesh,
        in_specs=placed,
        out_specs=(
            P(("peer", "grp"), None),
            P(("peer", "grp"), None),
            P(("peer", "grp"), None),
            P("peer", None),
            P("peer", None, "grp"),
        ),
        check_vma=False,
    )
```

profile of v0, /device:TPU:1, one launch (start us, length us, event | category | flops | bytes accessed | tf_op | source)
XLA Modules:
  0.0 241.6 jit_solution(15468367893541020206)
XLA Ops:
  0.6 0.0 copy-start
  0.6 0.0 copy-start.9
  0.7 0.0 copy-start.10
  0.7 0.8 convert_reduce_fusion.2
  1.4 0.1 copy.39
  1.6 0.2 reduce_window_sum.11
  1.7 0.1 copy.44
  1.8 1.4 convolution_convert_fusion.1
  3.2 1.6 broadcast_in_dim.60
  4.7 11.0 %all-to-all-start = ((bf16[16,2,16,2048]{3,2,1,0:T(8,128)(2,1)}), bf16[16,2,16,2048]{3,2,1,0:T(8,128)(2,1)}, u32[]{:S(2)}, u32[]{:S(2)}) async-start(bf16[16,2,16,2048]{3,2,1,0:T(8,128)(2,1)} %bitcast.4), calls=%async_computation | async-start | bytes 4194304 | tf_op jit(solution)/shard_map/all_to_all | solution.py:116
  15.8 0.0 copy-done.9
  15.8 0.0 copy-done.10
  15.8 0.1 fusion.36
  15.9 0.0 copy-done.3
  15.9 0.3 fusion.1
  16.3 28.3 %all-to-all-done = bf16[16,2,16,2048]{3,2,1,0:T(8,128)(2,1)} async-done(((bf16[16,2,16,2048]{3,2,1,0:T(8,128)(2,1)}), bf16[16,2,16,2048]{3,2,1,0:T(8,128)(2,1)}, u32[]{:S(2)}, u32[]{:S(2)}) %all-to-all-start) | async-done | bytes 2097184 | tf_op jit(solution)/shard_map/all_to_all | solution.py:116
  44.6 1.6 broadcast_in_dim.63
  46.1 5.5 %all-to-all-start.2 = ((bf16[16,2,16,2048]{3,2,1,0:T(8,128)(2,1)}), bf16[16,2,16,2048]{3,2,1,0:T(8,128)(2,1)S(1)}, u32[]{:S(2)}, u32[]{:S(2)}) async-start(bf16[16,2,16,2048]{3,2,1,0:T(8,128)(2,1)} %bitcast.17), calls=%async_computation.2 | async-start | bytes 4194304 | tf_op jit(solution)/shard_map/all_to_all | solution.py:117
  51.6 0.0 copy-done
  51.6 3.2 %fusion.10 = f32[512,176]{0,1:T(8,128)} fusion(bf16[512,2048]{1,0:T(8,128)(2,1)} %bitcast.5, bf16[1,2048,176]{1,2,0:T(8,128)(2,1)S(1)} %copy-done), kind=kOutput, calls=%fused_computation.23 | convolution fusion | flops 369098752 | bytes 3178496 | tf_op jit(solution)/shard_map/dot_general | solution.py:26
  54.9 0.0 copy-done.6
  54.9 3.2 %fusion.6 = f32[512,176]{0,1:T(8,128)} fusion(bf16[512,2048]{1,0:T(8,128)(2,1)} %bitcast.5, bf16[1,2048,176]{1,2,0:T(8,128)(2,1)S(1)} %copy-done.6), kind=kOutput, calls=%fused_computation.19 | convolution fusion | flops 369098752 | bytes 3178496 | tf_op jit(solution)/shard_map/dot_general | solution.py:27
  58.1 22.1 %all-to-all-done.2 = bf16[16,2,16,2048]{3,2,1,0:T(8,128)(2,1)S(1)} async-done(((bf16[16,2,16,2048]{3,2,1,0:T(8,128)(2,1)}), bf16[16,2,16,2048]{3,2,1,0:T(8,128)(2,1)S(1)}, u32[]{:S(2)}, u32[]{:S(2)}) %all-to-all-start.2) | async-done | bytes 2097184 | tf_op jit(solution)/shard_map/all_to_all | solution.py:117
  80.2 2.1 fusion.2
  82.3 0.0 copy-done.4
  82.3 0.0 copy-done.8
  82.3 0.8 fusion.8
  83.1 0.0 copy-done.7
  83.1 2.1 add_convert_fusion
  85.2 5.5 %all-to-all-start.3 = ((bf16[16,2,16,2048]{3,2,1,0:T(8,128)(2,1)}), bf16[16,2,16,2048]{3,2,1,0:T(8,128)(2,1)S(1)}, u32[]{:S(2)}, u32[]{:S(2)}) async-start(bf16[16,2,16,2048]{3,2,1,0:T(8,128)(2,1)} %bitcast.88), calls=%async_computation.3 | async-start | bytes 4194304 | tf_op jit(solution)/shard_map/all_to_all | solution.py:126
  90.7 1.9 collective-permute-start
  92.7 0.1 copy.41
  92.8 0.1 reshape.164
  92.9 0.0 copy-start.11
  92.9 3.8 %gather_fusion = s32[512]{0:T(512)S(1)} fusion(s32[128,4]{1,0:T(8,128)S(1)} %sub.61, s32[512]{0:T(512)S(1)} %reshape.164), kind=kCustom, calls=%fused_computation.2 | custom fusion | bytes 8192 | tf_op jit(solution)/shard_map/jit(take_along_axis)/gather | solution.py:136
  96.7 0.1 reshape.167
  96.8 0.1 copy.42
  96.9 1.2 convert_element_type.80
  98.1 0.1 copy.37
  98.2 0.1 copy.45
  98.3 0.1 reshape.179
  98.4 0.1 copy.38
  98.5 1.1 reduce_max.28
  99.7 6.6 %collective-permute-done = bf16[1,8,9496]{2,1,0:T(8,128)(2,1)} collective-permute-done((bf16[1,8,9496]{2,1,0:T(8,128)(2,1)}, bf16[1,8,9496]{2,1,0:T(8,128)(2,1)}, u32[]{:S(2)}, u32[]{:S(2)}) %collective-permute-start) | collective-permute-done | bytes 151968 | tf_op jit(solution)/shard_map/ppermute | solution.py:13
  106.3 1.1 reduce_max.30
  107.4 0.1 copy.43
  107.5 37.9 %all-reduce.1 = (f32[8]{0:T(128)S(1)}, f32[8]{0:T(128)S(1)}) all-reduce(bf16[8]{0:T(256)(128)(2,1)S(1)} %reduce_max.30, bf16[8]{0:T(256)(128)(2,1)S(1)} %reduce_max.28), channel_id=1, replica_groups=mesh['peer'=32,'grp'=16] {'grp'}, use_global_device_ids=true, to_apply=%region_15.17 | all-reduce | flops 16 | bytes 96 | tf_op jit(solution)/shard_map/pmax | solution.py:61
  145.5 1.4 fusion.19
  146.8 34.1 %all-reduce = (f32[8]{0:T(128)S(1)}, f32[8]{0:T(128)S(1)}, f32[8]{0:T(128)S(1)}, f32[8]{0:T(128)S(1)}) all-reduce(f32[8]{0:T(128)S(1)} %get-tuple-element.22, f32[8]{0:T(128)S(1)} %get-tuple-element.23, f32[8]{0:T(128)S(1)} %get-tuple-element.21, f32[8]{0:T(128)S(1)} %get-tuple-element.20), channel_id=1, replica_groups=mesh['peer'=32,'grp'=16] {'grp'}, use_global_device_ids=true, to_apply=%region_19.21 | all-reduce | flops 32 | bytes 256 | tf_op jit(solution)/shard_map/psum | solution.py:66
  181.0 0.5 subtract_bitcast_fusion
  181.5 3.5 %convolution_convert_fusion = bf16[512,2048]{1,0:T(8,128)(2,1)} fusion(bf16[1,176,2048]{2,1,0:T(8,128)(2,1)} %param.18, f32[512,176]{0,1:T(8,128)} %fusion.6, f32[512,176]{0,1:T(8,128)} %fusion.10), kind=kOutput, calls=%fused_computation.11 | convolution fusion | flops 370688000 | bytes 3538944 | tf_op jit(solution)/shard_map/dot_general | solution.py:29
  185.0 0.0 all-to-all-done.3
  185.0 4.8 %all-to-all-start.1 = ((bf16[16,2,16,2048]{3,2,1,0:T(8,128)(2,1)}), bf16[16,2,16,2048]{3,2,1,0:T(8,128)(2,1)}, u32[]{:S(2)}, u32[]{:S(2)}) async-start(bf16[16,2,16,2048]{3,2,1,0:T(8,128)(2,1)} %bitcast.89), calls=%async_computation.1 | async-start | bytes 4194304 | tf_op jit(solution)/shard_map/all_to_all | solution.py:125
  189.8 1.8 fusion.25
  191.6 2.1 convert_reduce_fusion
  193.7 3.6 %gather_fusion.2 = f32[512,2048]{1,0:T(8,128)} fusion(f32[128,2048]{1,0:T(8,128)S(1)} %bitcast.86, s32[1024]{0:T(1024)S(1)} %pad_clamp_fusion), kind=kCustom, calls=%fused_computation.1.clone | custom fusion | bytes 8390656 | tf_op jit(solution)/shard_map/jit(_take)/gather | solution.py:145
  197.3 5.2 %reshape.186 = f32[128,4,2048]{2,1,0:T(4,128)} reshape(f32[512,2048]{1,0:T(8,128)} %gather_fusion.2) | data formatting | bytes 8388608 | tf_op jit(solution)/shard_map/jit(_take)/gather | solution.py:145
  202.5 16.1 %all-to-all-done.1 = bf16[16,2,16,2048]{3,2,1,0:T(8,128)(2,1)} async-done(((bf16[16,2,16,2048]{3,2,1,0:T(8,128)(2,1)}), bf16[16,2,16,2048]{3,2,1,0:T(8,128)(2,1)}, u32[]{:S(2)}, u32[]{:S(2)}) %all-to-all-start.1) | async-done | bytes 2097184 | tf_op jit(solution)/shard_map/all_to_all | solution.py:125
  218.6 2.1 convert_reduce_fusion.1
  220.7 3.6 %gather_fusion.1 = f32[512,2048]{1,0:T(8,128)} fusion(f32[128,2048]{1,0:T(8,128)S(1)} %bitcast.85, s32[1024]{0:T(1024)S(1)} %pad_clamp_fusion), kind=kCustom, calls=%fused_computation.clone | custom fusion | bytes 8390656 | tf_op jit(solution)/shard_map/jit(_take)/gather | solution.py:140
  224.3 5.3 %reshape.182 = f32[128,4,2048]{2,1,0:T(4,128)} reshape(f32[512,2048]{1,0:T(8,128)} %gather_fusion.1) | data formatting | bytes 8388608 | tf_op jit(solution)/shard_map/jit(_take)/gather | solution.py:140
  229.5 0.0 copy-done.2
  229.5 11.4 %multiply_reduce_fusion = (f32[128,4]{1,0:T(8,128)S(1)}, bf16[128,2048]{1,0:T(8,128)(2,1)}, bf16[128,2048]{1,0:T(8,128)(2,1)}) fusion(f32[128,4,2048]{2,1,0:T(4,128)} %reshape.182, f32[128,2048]{1,0:T(8,128)S(1)} %copy-done.2, pred[128,4]{1,0:T(8,128)(4,1)S(1)} %copy.43, pred[128,4]{1,0:T(8,128)(4,1)S(1)} %copy.38, f32[128,4]{1,0:T(8,128)S(1)} %copy.37, ...), kind=kLoop, calls=%fused_computation.8 | loop fusion | flops 8912384 | bytes 10490880 | tf_op jit(solution)/shard_map/reduce_sum | solution.py:149
  240.9 0.7 copy.48
  (18 shorter events, 0.1 us)
Async XLA Ops:
  0.6 51.0 %copy-start = (bf16[1,2048,176]{1,2,0:T(8,128)(2,1)S(1)}, bf16[1,2048,176]{1,2,0:T(8,128)(2,1)}, u32[]{:S(2)}) copy-start(bf16[1,2048,176]{1,2,0:T(8,128)(2,1)} %param.16) | copy-start | bytes 2162692
  0.6 15.1 %copy-start.9 = (s32[128,4]{0,1:T(4,128)S(1)}, s32[128,4]{0,1:T(4,128)}, u32[]{:S(2)}) copy-start(s32[128,4]{0,1:T(4,128)} %param.14) | copy-start | bytes 6148
  0.7 15.1 %copy-start.10 = (f32[128,4]{0,1:T(4,128)S(1)}, f32[128,4]{0,1:T(4,128)}, u32[]{:S(2)}) copy-start(f32[128,4]{0,1:T(4,128)} %param.15) | copy-start | bytes 6148
  1.4 14.5 %copy-start.3 = (bf16[128,2048]{1,0:T(8,128)(2,1)S(1)}, bf16[128,2048]{1,0:T(8,128)(2,1)}, u32[]{:S(2)}) copy-start(bf16[128,2048]{1,0:T(8,128)(2,1)} %param.13) | copy-start | bytes 1572868
  4.7 39.8 %all-to-all-start = ((bf16[16,2,16,2048]{3,2,1,0:T(8,128)(2,1)}), bf16[16,2,16,2048]{3,2,1,0:T(8,128)(2,1)}, u32[]{:S(2)}, u32[]{:S(2)}) async-start(bf16[16,2,16,2048]{3,2,1,0:T(8,128)(2,1)} %bitcast.4), calls=%async_computation | async-start | bytes 4194304 | tf_op jit(solution)/shard_map/all_to_all | solution.py:116
  46.1 34.1 %all-to-all-start.2 = ((bf16[16,2,16,2048]{3,2,1,0:T(8,128)(2,1)}), bf16[16,2,16,2048]{3,2,1,0:T(8,128)(2,1)S(1)}, u32[]{:S(2)}, u32[]{:S(2)}) async-start(bf16[16,2,16,2048]{3,2,1,0:T(8,128)(2,1)} %bitcast.17), calls=%async_computation.2 | async-start | bytes 4194304 | tf_op jit(solution)/shard_map/all_to_all | solution.py:117
  51.6 3.3 %copy-start.6 = (bf16[1,2048,176]{1,2,0:T(8,128)(2,1)S(1)}, bf16[1,2048,176]{1,2,0:T(8,128)(2,1)}, u32[]{:S(2)}) copy-start(bf16[1,2048,176]{1,2,0:T(8,128)(2,1)} %param.17) | copy-start | bytes 2162692
  80.2 2.1 copy-start.4
  80.2 2.1 copy-start.8
  80.2 2.9 %copy-start.7 = (bf16[1,2048,176]{1,2,0:T(8,128)(2,1)S(1)}, bf16[1,2048,176]{1,2,0:T(8,128)(2,1)}, u32[]{:S(2)}) copy-start(bf16[1,2048,176]{1,2,0:T(8,128)(2,1)} %param.17) | copy-start | bytes 2162692
  85.2 99.7 %all-to-all-start.3 = ((bf16[16,2,16,2048]{3,2,1,0:T(8,128)(2,1)}), bf16[16,2,16,2048]{3,2,1,0:T(8,128)(2,1)S(1)}, u32[]{:S(2)}, u32[]{:S(2)}) async-start(bf16[16,2,16,2048]{3,2,1,0:T(8,128)(2,1)} %bitcast.88), calls=%async_computation.3 | async-start | bytes 4194304 | tf_op jit(solution)/shard_map/all_to_all | solution.py:126
  90.7 15.6 %collective-permute-start = (bf16[1,8,9496]{2,1,0:T(8,128)(2,1)}, bf16[1,8,9496]{2,1,0:T(8,128)(2,1)}, u32[]{:S(2)}, u32[]{:S(2)}) collective-permute-start(bf16[1,8,9496]{2,1,0:T(8,128)(2,1)} %param.20), channel_id=1, source_target_pairs={{0,16},{16,32},{32,48},{48,64},{64,80},{80,96},{96,112},{112,128},... | collective-permute-start | bytes 455816 | tf_op jit(solution)/shard_map/ppermute | solution.py:13
  92.9 52.6 %copy-start.11 = (s32[1,8]{1,0:T(1,128)S(1)}, s32[1,8]{1,0:T(1,128)}, u32[]{:S(2)}) copy-start(s32[1,8]{1,0:T(1,128)} %param.21) | copy-start | bytes 100
  99.6 90.2 %copy-start.5 = (bf16[1,8,9496]{2,1,0:T(8,128)(2,1)S(1)}, bf16[1,8,9496]{2,1,0:T(8,128)(2,1)}, u32[]{:S(2)}) copy-start(bf16[1,8,9496]{2,1,0:T(8,128)(2,1)} %param.19) | copy-start | bytes 455812
  185.0 6.6 %copy-start.1 = (bf16[16,2,16,2048]{3,2,1,0:T(8,128)(2,1)}, bf16[16,2,16,2048]{3,2,1,0:T(8,128)(2,1)S(1)}, u32[]{:S(2)}) copy-start(bf16[16,2,16,2048]{3,2,1,0:T(8,128)(2,1)S(1)} %all-to-all-done.3) | copy-start | bytes 6291460
  185.0 33.6 %all-to-all-start.1 = ((bf16[16,2,16,2048]{3,2,1,0:T(8,128)(2,1)}), bf16[16,2,16,2048]{3,2,1,0:T(8,128)(2,1)}, u32[]{:S(2)}, u32[]{:S(2)}) async-start(bf16[16,2,16,2048]{3,2,1,0:T(8,128)(2,1)} %bitcast.89), calls=%async_computation.1 | async-start | bytes 4194304 | tf_op jit(solution)/shard_map/all_to_all | solution.py:125
  224.3 5.3 %copy-start.2 = (f32[128,2048]{1,0:T(8,128)S(1)}, f32[128,2048]{1,0:T(8,128)}, u32[]{:S(2)}) copy-start(f32[128,2048]{1,0:T(8,128)} %convert_element_type.80) | copy-start | bytes 3145732
where the time goes:
time: 242 us
  waiting for transfers between devices  73.2 us (30%)
  blocking collectives  72.1 us (30%)
  starting transfers between devices  28.7 us (12%)
  local copies, waits for them, and re-layouts  26.4 us (11%)
  other arithmetic  23.6 us (10%)
  matrix products  16.7 us (7%)
    pmax x1, blocking collectives, distill(): max_student, max_teacher = lax.pmax((local_smax, local_tmax), 'grp')  37.9 us
    psum x1, blocking collectives, distill(): lax.psum((student_exp, teacher_sum, cross_sum, label_logit), 'grp')  34.1 us
    all_to_all x1, waiting for transfers between devices, body(): lax.all_to_all(send_rows, 'grp', split_axis=0, concat_axis=0, tiled=True)  28.3 us
    all_to_all x1, waiting for transfers between devices, body(): lax.all_to_all(send_scaled, 'grp', split_axis=0, concat_axis=0, tiled=True)  22.1 us
    all_to_all x1, waiting for transfers between devices, body(): lax.all_to_all(piece_out, 'grp', split_axis=0, concat_axis=0, tiled=True)  16.1 us
    reduce_sum x1, other arithmetic, body(): jnp.sum(cotangent.astype(jnp.float32)[:, None, :] * out_rows, axis=2)  11.4 us
    all_to_all x1, starting transfers between devices, body(): lax.all_to_all(send_rows, 'grp', split_axis=0, concat_axis=0, tiled=True)  11 us
    gather x2, local copies, waits for them, and re-layouts, body(): jnp.take(expert_out.reshape(-1, model_width), flat_index, axis=0)  8.82 us
  transfers between devices with their start and end apart: 5, of which 4 were waited for; matrix products, arithmetic and copies ran while one was open for 14% of the time, Pallas kernels for 0%

commit v1 on v0

v1 whole, which is shorter than its diff:
```python
import functools

import jax
import jax.numpy as jnp
from jax import lax
from jax.experimental import pallas as pl
from jax.experimental.pallas import tpu as pltpu
from jax.sharding import PartitionSpec as P

MESH = pl.DeviceIdType.MESH
CAP = 32
CHIPS = 8
BATCHES = ((0,), (6,), (1, 7), (3, 5), (4, 2))
ORDER = tuple(r for batch in BATCHES for r in batch)
F32 = jnp.float32
BF16 = jnp.bfloat16
NT = (((1,), (1,)), ((), ()))


def dot(a, b):
    return jnp.dot(a, b, preferred_element_type=F32)


def dot_nt(a, b):
    return lax.dot_general(a, b, NT, preferred_element_type=F32)


def kernel(
    tok_h, cot_h, ids_h, prob_h, wg_h, wu_h, wd_h, stu_h, sta_h, lab_h,
    lay_h, ing_h, pgr_h, loss_h, lgr_h,
    tok, cot, ids, prob, wg, wu, wd, stu, tea, lab,
    lay, ing, pgr, loss, lgr,
    send, take, part, back, stat, in_sem, out_sem, far_send, far_recv, w_send, w_recv,
    d_send, d_recv, r_send, r_recv, s_send, s_recv, t_send, t_recv,
):
    peer, grp = lax.axis_index("peer"), lax.axis_index("grp")
    n_peer, n_grp = lax.axis_size("peer"), lax.axis_size("grp")
    chip, core = grp // 2, grp % 2
    twin = (peer, chip * 2 + (1 - core))
    after = (lax.rem(peer + 1, n_peer), grp)
    before = (lax.rem(peer + n_peer - 1, n_peer), grp)

    def xor(a, bits, width):
        out = a
        for b in range(width):
            if bits >> b & 1:
                out = out + (1 << b) * (1 - 2 * ((a // (1 << b)) % 2))
        return out

    def chip_at(r):
        return (peer, xor(chip, r, 3) * 2 + core)

    def member_at(k):
        return (peer, xor(grp, k, 4))

    barrier = pltpu.get_barrier_semaphore()
    for k in range(1, 16):
        pl.semaphore_signal(barrier, inc=1, device_id=member_at(k), device_id_type=MESH)
    pl.semaphore_signal(barrier, inc=1, device_id=after, device_id_type=MESH)
    pl.semaphore_signal(barrier, inc=1, device_id=before, device_id_type=MESH)

    loads = [
        pltpu.make_async_copy(src, dst, in_sem.at[i])
        for i, (src, dst) in enumerate(
            (
                (ids_h, ids), (prob_h, prob), (tok_h, tok), (cot_h, cot), (stu_h.at[0], stu), (lab_h, lab),
                (wg_h.at[0], wg), (wu_h.at[0], wu), (wd_h.at[0], wd),
            )
        )
    ]
    for copy in loads:
        copy.start()

    loads[0].wait()
    loads[1].wait()
    lanes = lax.broadcasted_iota(jnp.int32, (1, CHIPS * CAP), 1)
    own_expert = chip // 2
    lane_pair = lanes // (2 * CAP)
    lane_expert = (own_expert // 2 + lane_pair // 2) % 2 * 2 + (own_expert + lane_pair) % 2
    lane_slot = lanes % CAP
    hits = [ids[:, k : k + 1] == lane_expert for k in range(4)]
    member = functools.reduce(jnp.add, [h.astype(F32) for h in hits])
    rows = lax.broadcasted_iota(jnp.int32, (128, 128), 0)
    columns = lax.broadcasted_iota(jnp.int32, (128, 128), 1)
    earlier = (columns < rows).astype(F32).astype(BF16)
    position = dot(earlier, member.astype(BF16))
    chosen = jnp.where((member > 0.0) & (position.astype(jnp.int32) == lane_slot), 1.0, 0.0)
    weight = functools.reduce(
        jnp.add, [jnp.where(h, prob[:, k : k + 1], 0.0) for k, h in enumerate(hits)]
    ) * chosen
    picks = []
    for j in range(4):
        picks.append(slice(j * 2 * CAP, j * 2 * CAP + CAP))
    chosen_4 = jnp.concatenate([chosen[:, p] for p in picks], axis=1)
    weight_4 = jnp.concatenate([weight[:, p] for p in picks], axis=1)
    gather = chosen_4.T.astype(BF16)
    slot_prob = jnp.sum(weight_4.T, axis=1, keepdims=True)
    loads[2].wait()
    for n in range(0, 2048, 512):
        send[0, :, :, n : n + 512] = dot(gather, tok[:, n : n + 512]).astype(BF16).reshape(4, CAP, 512)
    loads[3].wait()
    for n in range(0, 2048, 512):
        send[1, :, :, n : n + 512] = (
            (slot_prob * dot(gather, cot[:, n : n + 512])).astype(BF16).reshape(4, CAP, 512)
        )

    pl.semaphore_wait(barrier, 17)

    def remote(src, dst, s, r, target):
        return pltpu.make_async_remote_copy(
            src_ref=src, dst_ref=dst, send_sem=s, recv_sem=r, device_id=target, device_id_type=MESH
        )

    spot = {r: i for i, r in enumerate(ORDER)}
    out_going = {
        r: remote(send.at[:, r // 2], take.at[:, spot[r]], d_send.at[r], d_recv.at[r], chip_at(r))
        for r in ORDER
        if r
    }
    returning = {
        r: remote(part.at[:, spot[r]], back.at[:, r], r_send.at[r], r_recv.at[r], chip_at(r))
        for r in ORDER
        if r
    }
    swaps = [
        remote(src, dst, w_send.at[i], w_recv.at[i], twin)
        for i, (src, dst) in enumerate(
            ((wg_h.at[0], far_send.at[0]), (wu_h.at[0], far_send.at[1]), (wd_h.at[0], far_recv))
        )
    ]
    teacher_copy = remote(sta_h.at[0], tea, t_send, t_recv, after)
    for r in ORDER:
        if r:
            out_going[r].start()
    for copy in swaps:
        copy.start()
    teacher_copy.start()

    take[:, 0] = send[:, 0]

    loads[4].wait()
    loads[5].wait()
    teacher_copy.wait_recv()
    eye = lax.broadcasted_iota(jnp.int32, (8, 8), 0) == lax.broadcasted_iota(jnp.int32, (8, 8), 1)
    label = jnp.sum(jnp.where(eye, lab[...].astype(F32), 0.0), axis=1, keepdims=True).astype(jnp.int32)
    student = stu[...].astype(F32)
    teacher = tea[...].astype(F32)
    width = student.shape[1]
    vocab = grp * width + lax.broadcasted_iota(jnp.int32, student.shape, 1)
    lane = lax.broadcasted_iota(jnp.int32, (8, 128), 1)
    top_s = jnp.max(student, axis=1, keepdims=True)
    top_t = jnp.max(teacher, axis=1, keepdims=True)
    exp_t = jnp.exp(teacher - top_t)
    stats = (
        top_s,
        top_t,
        jnp.sum(jnp.exp(student - top_s), axis=1, keepdims=True),
        jnp.sum(exp_t, axis=1, keepdims=True),
        jnp.sum(exp_t * (teacher - student), axis=1, keepdims=True),
        jnp.sum(jnp.where(vocab == label, student, 0.0), axis=1, keepdims=True),
    )
    stat[0] = functools.reduce(
        jnp.add, [jnp.where(lane == i, s, 0.0) for i, s in enumerate(stats)]
    )
    telling = [
        remote(stat.at[0], stat.at[k], s_send.at[k], s_recv.at[k], member_at(k)) for k in range(1, 16)
    ]
    for copy in telling:
        copy.start()

    for copy in loads[6:]:
        copy.wait()
    for copy in swaps:
        copy.wait()
    halves = ((wg, wu, wd), (far_send.at[0], far_send.at[1], far_recv))
    for batch in BATCHES:
        for r in batch:
            if r:
                out_going[r].wait_recv()
        first, count = spot[batch[0]], len(batch)
        x = take[0, first : first + count].reshape(count * CAP, 2048)
        s = take[1, first : first + count].reshape(count * CAP, 2048)
        inner = []
        for gate_w, up_w, down_w in halves:
            gate = dot(x, gate_w[...])
            up = dot(x, up_w[...])
            grad = dot_nt(s, down_w[...])
            sig = jax.nn.sigmoid(gate)
            hidden = (gate * sig * up).astype(BF16)
            grad_gate = (grad * up * sig * (1.0 + gate * (1.0 - sig))).astype(BF16)
            grad_up = (grad * gate * sig).astype(BF16)
            inner.append((hidden, grad_gate, grad_up))
        for n in range(0, 2048, 512):
            cut = slice(n, n + 512)
            out_piece = functools.reduce(
                jnp.add, [dot(i[0], h[2][:, cut]) for i, h in zip(inner, halves)]
            )
            grad_piece = functools.reduce(
                jnp.add,
                [dot_nt(i[1], h[0][cut, :]) + dot_nt(i[2], h[1][cut, :]) for i, h in zip(inner, halves)],
            )
            for kind, value in ((0, out_piece), (1, grad_piece)):
                value = value.astype(BF16).reshape(count, CAP, 512)
                if batch == (0,):
                    back[kind, 0, :, cut] = value[0]
                else:
                    part[kind, first : first + count, :, cut] = value
        for r in batch:
            if r:
                returning[r].start()

    for copy in telling:
        copy.wait()
    seen = [stat[k] for k in range(16)]
    def col(k, i):
        return seen[k][:, i : i + 1]
    max_s = functools.reduce(jnp.maximum, [col(k, 0) for k in range(16)])
    max_t = functools.reduce(jnp.maximum, [col(k, 1) for k in range(16)])
    scale_s = [jnp.exp(col(k, 0) - max_s) for k in range(16)]
    scale_t = [jnp.exp(col(k, 1) - max_t) for k in range(16)]
    sum_s = functools.reduce(jnp.add, [col(k, 2) * scale_s[k] for k in range(16)])
    sum_t = functools.reduce(jnp.add, [col(k, 3) * scale_t[k] for k in range(16)])
    cross = functools.reduce(jnp.add, [col(k, 4) * scale_t[k] for k in range(16)])
    label_logit = functools.reduce(jnp.add, [col(k, 5) for k in range(16)])
    lse_s = max_s + jnp.log(sum_s)
    lse_t = max_t + jnp.log(sum_t)
    value = 2.0 * lse_s - label_logit + cross / sum_t - lse_t
    loss[...] = jnp.sum(jnp.where(eye, value, 0.0), axis=0, keepdims=True)
    student = stu[...].astype(F32)
    teacher = tea[...].astype(F32)
    onehot = jnp.where(vocab == label, 1.0, 0.0)
    lgr[...] = (2.0 * jnp.exp(student - lse_s) - onehot - jnp.exp(teacher - lse_t)).astype(BF16)

    for r in ORDER:
        if r:
            returning[r].wait_recv()
    weight_hi = weight.astype(BF16)
    weight_lo = (weight - weight_hi.astype(F32)).astype(BF16)
    chosen_bf = chosen.astype(BF16)
    out_rows = back[0].reshape(CHIPS * CAP, 2048)
    inner_product = dot_nt(cot[...], out_rows) * chosen
    lane4 = lax.broadcasted_iota(jnp.int32, (128, 4), 1)
    pgr[...] = functools.reduce(
        jnp.add,
        [
            jnp.where(lane4 == k, jnp.sum(jnp.where(h, inner_product, 0.0), axis=1, keepdims=True), 0.0)
            for k, h in enumerate(hits)
        ],
    )
    for n in range(0, 2048, 512):
        cut = slice(n, n + 512)
        rows_n = back[0, :, :, cut].reshape(CHIPS * CAP, 512)
        lay[:, cut] = (dot(weight_hi, rows_n) + dot(weight_lo, rows_n)).astype(BF16)
        ing[:, cut] = dot(chosen_bf, back[1, :, :, cut].reshape(CHIPS * CAP, 512)).astype(BF16)
    stores = [
        pltpu.make_async_copy(src, dst, out_sem.at[i])
        for i, (src, dst) in enumerate(
            ((lay, lay_h), (ing, ing_h), (pgr, pgr_h), (loss, loss_h), (lgr, lgr_h.at[0]))
        )
    ]
    for copy in stores:
        copy.start()
    teacher_copy.wait_send()
    for r in ORDER:
        if r:
            out_going[r].wait_send()
            returning[r].wait_send()
    for copy in stores:
        copy.wait()


def body(*args):
    tokens, cotangent, expert_ids, route_prob, w_gate, w_up, w_down, student, stale, labels = args
    width = student.shape[2]
    dma = pltpu.SemaphoreType.DMA
    return pl.pallas_call(
        kernel,
        name="layer",
        out_shape=(
            jax.ShapeDtypeStruct(tokens.shape, BF16),
            jax.ShapeDtypeStruct(tokens.shape, BF16),
            jax.ShapeDtypeStruct(route_prob.shape, F32),
            jax.ShapeDtypeStruct(labels.shape, F32),
            jax.ShapeDtypeStruct(student.shape, BF16),
        ),
        in_specs=[pl.BlockSpec(memory_space=pl.ANY)] * 10,
        out_specs=[pl.BlockSpec(memory_space=pl.ANY)] * 5,
        scratch_shapes=[
            pltpu.VMEM(tokens.shape, BF16),
            pltpu.VMEM(tokens.shape, BF16),
            pltpu.VMEM(expert_ids.shape, jnp.int32),
            pltpu.VMEM(route_prob.shape, F32),
            pltpu.VMEM(w_gate.shape[1:], BF16),
            pltpu.VMEM(w_up.shape[1:], BF16),
            pltpu.VMEM(w_down.shape[1:], BF16),
            pltpu.VMEM((8, width), BF16),
            pltpu.VMEM((8, width), BF16),
            pltpu.VMEM(labels.shape, jnp.int32),
            pltpu.VMEM(tokens.shape, BF16),
            pltpu.VMEM(tokens.shape, BF16),
            pltpu.VMEM(route_prob.shape, F32),
            pltpu.VMEM(labels.shape, F32),
            pltpu.VMEM((8, width), BF16),
            pltpu.VMEM((2, 4, CAP, 2048), BF16),
            pltpu.VMEM((2, CHIPS, CAP, 2048), BF16),
            pltpu.VMEM((2, CHIPS, CAP, 2048), BF16),
            pltpu.VMEM((2, CHIPS, CAP, 2048), BF16),
            pltpu.VMEM((16, 8, 128), F32),
            dma((9,)),
            dma((5,)),
            pltpu.VMEM((2,) + w_gate.shape[1:], BF16),
            pltpu.VMEM(w_down.shape[1:], BF16),
            dma((3,)),
            dma((3,)),
            dma((8,)),
            dma((8,)),
            dma((8,)),
            dma((8,)),
            dma((16,)),
            dma((16,)),
            dma,
            dma,
        ],
        compiler_params=pltpu.CompilerParams(
            collective_id=0, has_side_effects=True, vmem_limit_bytes=56 << 20
        ),
    )(*args)


def solution(mesh):
    rows = P(("peer", "grp"), None)
    vocab = P("peer", None, "grp")
    peer_row = P("peer", None)
    return jax.shard_map(
        body,
        mesh=mesh,
        in_specs=(
            rows, rows, rows, rows, vocab, vocab, P("peer", "grp", None), vocab, vocab, peer_row,
        ),
        out_specs=(rows, rows, rows, peer_row, vocab),
        check_vma=False,
    )
```

time: 242 us -> 82.8 us (0.34)
  waiting for transfers between devices: 73.2 us -> 0 us
  blocking collectives: 72.1 us -> 0 us
  Pallas kernels: 0 us -> 70.8 us
  starting transfers between devices: 28.7 us -> 0 us
  other arithmetic: 23.6 us -> 0 us
  matrix products: 16.7 us -> 0 us
  local copies, waits for them, and re-layouts: 26.4 us -> 11.1 us
    pallas_call x0 -> x1, Pallas kernels: none -> 70.8 us  [body(): pl.pallas_call(kernel, name='layer', out_shape=(jax.ShapeDtypeStruct(toke...]
    all_to_all x4 -> x0, waiting for transfers between devices: 66.5 us -> none  [the longest x1 28.3 us: body(): lax.all_to_all(send_rows, 'grp', split_axis=0, concat_axis=0, tiled=True)]
    pmax x1 -> x0, blocking collectives: 37.9 us -> none  [distill(): max_student, max_teacher = lax.pmax((local_smax, local_tmax), 'grp')]
    psum x1 -> x0, blocking collectives: 34.1 us -> none  [distill(): lax.psum((student_exp, teacher_sum, cross_sum, label_logit), 'grp')]
    all_to_all x4 -> x0, starting transfers between devices: 26.8 us -> none  [the longest x1 11 us: body(): lax.all_to_all(send_rows, 'grp', split_axis=0, concat_axis=0, tiled=True)]
    gather x9 -> x0, local copies, waits for them, and re-layouts: 21.8 us -> none  [the longest x2 8.82 us: body(): jnp.take(expert_out.reshape(-1, model_width), flat_index, axis=0)]
    reduce_sum x6 -> x0, other arithmetic: 17.7 us -> none  [the longest x1 11.4 us: body(): jnp.sum(cotangent.astype(jnp.float32)[:, None, :] * out_rows, axis=2)]
    dot_general x9 -> x0, matrix products: 16.7 us -> none  [the longest x1 3.49 us: forward_piece(): jnp.dot(hidden, down_rows, preferred_element_type=jnp.float32)]
  transfers between devices with their start and end apart: 5 -> 0, of which waited for: 4 -> 0; matrix products, arithmetic and copies ran while one was open for 14% -> 0% of each run, Pallas kernels for 0% -> 0%
where the time goes in v1:
time: 82.8 us; the launch traced here: 82.6 us
  Pallas kernels  70.8 us (86%)
  local copies, waits for them, and re-layouts  11.1 us (13%)
    pallas_call x1, Pallas kernels, body(): pl.pallas_call(kernel, name='layer', out_shape=(jax.ShapeDtypeStruct(toke...  70.8 us
    unnamed x18, local copies, waits for them, and re-layouts  9.65 us

profile of v1, /device:TPU:1, one launch (start us, length us, event | category | flops | bytes accessed | tf_op | source)
XLA Modules:
  0.0 82.6 jit_solution(6153308501770256899)
XLA Ops:
  0.6 0.0 copy-start.3
  0.6 1.4 %copy.15.ids_h = s32[128,4]{1,0:T(8,128)} copy(s32[128,4]{0,1:T(4,128)} %param.12) | data formatting | bytes 4096 | tf_op args[2]
  2.1 0.0 copy-done.3
  2.1 0.7 copy.16.prob_h
  2.8 0.0 copy-start
  2.8 2.3 %copy.17.wg_h = bf16[1,2048,176]{2,1,0:T(8,128)(2,1)} copy(bf16[1,2048,176]{1,2,0:T(8,128)(2,1)} %param.14) | data formatting | bytes 1441792 | tf_op args[4]
  5.1 0.0 copy-done
  5.1 1.3 %copy.18.wu_h = bf16[1,2048,176]{2,1,0:T(8,128)(2,1)} copy(bf16[1,2048,176]{1,2,0:T(8,128)(2,1)S(1)} %copy-done) | data formatting | bytes 1441792 | tf_op args[5]
  6.4 70.8 %layer.1 = (bf16[128,2048]{1,0:T(8,128)(2,1)}, bf16[128,2048]{1,0:T(8,128)(2,1)}, f32[128,4]{1,0:T(8,128)}, f32[1,8]{1,0:T(1,128)}, bf16[1,8,9496]{2,1,0:T(8,128)(2,1)}) custom-call(bf16[128,2048]{1,0:T(8,128)(2,1)} %tok_h.1, bf16[128,2048]{1,0:T(8,128)(2,1)} %cot_h.1, s32[128,4]{1,0:T(8,128)} %copy.15.ids_h, f32[128,4]{1,0:T(8,128)} %copy.16.prob_h, ...), custom_call_target="tpu_custom_call" | custom-call | tf_op jit(solution)/shard_map/layer/pallas_call | solution.py:276
  77.2 1.5 %copy.19 = f32[128,4]{0,1:T(4,128)} copy(f32[128,4]{1,0:T(8,128)} %get-tuple-element.7) | data formatting | bytes 4096 | tf_op jit(solution)/shard_map/layer/pallas_call | solution.py:276
  78.7 0.0 copy-start.1
  78.7 1.9 %copy.24 = bf16[128,2048]{1,0:T(8,128)(2,1)} copy(bf16[128,2048]{1,0:T(8,128)(2,1)} %get-tuple-element.15) | data formatting | bytes 1048576
  80.6 0.0 copy-done.1
  80.6 0.0 copy-start.4
  80.6 0.0 copy-start.2
  80.6 0.8 copy.25
  81.4 0.0 copy-done.4
  81.4 0.5 copy.26
  81.9 0.0 copy-done.2
  81.9 0.7 copy.27
Async XLA Ops:
  0.6 1.4 %copy-start.3 = (f32[128,4]{0,1:T(4,128)S(1)}, f32[128,4]{0,1:T(4,128)}, u32[]{:S(2)}) copy-start(f32[128,4]{0,1:T(4,128)} %param.13) | copy-start | bytes 6148
  2.8 2.3 %copy-start = (bf16[1,2048,176]{1,2,0:T(8,128)(2,1)S(1)}, bf16[1,2048,176]{1,2,0:T(8,128)(2,1)}, u32[]{:S(2)}) copy-start(bf16[1,2048,176]{1,2,0:T(8,128)(2,1)} %param.15) | copy-start | bytes 2162692
  78.7 1.9 %copy-start.1 = (bf16[128,2048]{1,0:T(8,128)(2,1)S(1)}, bf16[128,2048]{1,0:T(8,128)(2,1)}, u32[]{:S(2)}) copy-start(bf16[128,2048]{1,0:T(8,128)(2,1)} %get-tuple-element.16) | copy-start | bytes 1572868
  80.6 0.8 copy-start.4
  80.6 1.3 %copy-start.2 = (bf16[1,8,9496]{2,1,0:T(8,128)(2,1)S(1)}, bf16[1,8,9496]{2,1,0:T(8,128)(2,1)}, u32[]{:S(2)}) copy-start(bf16[1,8,9496]{2,1,0:T(8,128)(2,1)} %get-tuple-element.19) | copy-start | bytes 455812

commit v2 on v1

v2 whole, which is shorter than its diff:
```python
import functools

import jax
import jax.numpy as jnp
from jax import lax
from jax.experimental import pallas as pl
from jax.experimental.pallas import tpu as pltpu
from jax.sharding import PartitionSpec as P

MESH = pl.DeviceIdType.MESH
CAP = 32
CHIPS = 8
BATCHES = ((0,), (6,), (2, 4), (5, 3), (7, 1))
ORDER = tuple(r for batch in BATCHES for r in batch)
FAR = ORDER[1:]
SPOT = {r: i for i, r in enumerate(ORDER)}
SWAP_AT = 1
TELL_AT = 3
STEP = 512
F32 = jnp.float32
BF16 = jnp.bfloat16
NT = (((1,), (1,)), ((), ()))


def dot(a, b):
    return jnp.dot(a, b, preferred_element_type=F32)


def dot_nt(a, b):
    return lax.dot_general(a, b, NT, preferred_element_type=F32)


def total(terms):
    return functools.reduce(jnp.add, terms)


def xor(a, bits, width):
    out = a
    for b in range(width):
        if bits >> b & 1:
            out = out + (1 << b) * (1 - 2 * ((a // (1 << b)) % 2))
    return out


def slot_tables(ids, prob, chip):
    rows = lax.broadcasted_iota(jnp.int32, (CHIPS * CAP, 128), 0)
    row_spot = rows // CAP
    row_expert = total(
        [jnp.where(row_spot == i, xor(chip // 2, r // 2, 2), 0) for i, r in enumerate(ORDER)]
    )
    hits = [ids[k : k + 1, :] == row_expert for k in range(4)]
    member = total([h.astype(F32) for h in hits])
    earlier = (
        lax.broadcasted_iota(jnp.int32, (128, 128), 0) < lax.broadcasted_iota(jnp.int32, (128, 128), 1)
    )
    position = dot(member.astype(BF16), earlier.astype(F32).astype(BF16))
    chosen = jnp.where((member > 0.0) & (position.astype(jnp.int32) == rows % CAP), 1.0, 0.0)
    weight = total([jnp.where(h, prob[k : k + 1, :], 0.0) for k, h in enumerate(hits)]) * chosen
    return hits, chosen, weight


def logit_views(lab, width, grp):
    eye = lax.broadcasted_iota(jnp.int32, (8, 8), 0) == lax.broadcasted_iota(jnp.int32, (8, 8), 1)
    label = jnp.sum(jnp.where(eye, lab[...].astype(F32), 0.0), axis=1, keepdims=True).astype(jnp.int32)
    vocab = grp * width + lax.broadcasted_iota(jnp.int32, (8, width), 1)
    return eye, vocab == label


def expert_kernel(
    tok_h, cot_h, ids_h, prob_h, wg_h, wu_h, wd_h, stu_h, sta_h, lab_h,
    back_h, stat_h, tea_h,
    tok, cot, ids, prob, wg, wu, wd, stu, tea, lab, send, take, part, stat, twin_w, twin_d,
    in_sem, out_sem, w_send, w_recv, d_send, d_recv, r_send, r_recv, s_send, s_recv, t_send, t_recv,
):
    peer, grp = lax.axis_index("peer"), lax.axis_index("grp")
    n_peer = lax.axis_size("peer")
    chip, core = grp // 2, grp % 2
    twin = (peer, chip * 2 + (1 - core))
    depth = n_peer // 2
    half, z = peer // depth, lax.rem(peer, depth)
    after = (half * depth + lax.rem(z + 1, depth), grp)
    before = (half * depth + lax.rem(z + depth - 1, depth), grp)
    across = ((1 - half) * depth + z, grp)

    def chip_at(r):
        return (peer, xor(chip, r, 3) * 2 + core)

    def member_at(k):
        return (peer, xor(grp, k, 4))

    barrier = pltpu.get_barrier_semaphore()
    for k in range(1, 16):
        pl.semaphore_signal(barrier, inc=1, device_id=member_at(k), device_id_type=MESH)
    for near in (after, before, across):
        pl.semaphore_signal(barrier, inc=1, device_id=near, device_id_type=MESH)

    loads = [
        pltpu.make_async_copy(src, dst, in_sem.at[i])
        for i, (src, dst) in enumerate(
            (
                (ids_h, ids), (prob_h, prob), (tok_h, tok), (cot_h, cot), (stu_h.at[0], stu), (lab_h, lab),
                (wg_h.at[0], wg), (wu_h.at[0], wu), (wd_h.at[0], wd),
            )
        )
    ]
    for copy in loads:
        copy.start()

    def remote(src, dst, s, r, target):
        return pltpu.make_async_remote_copy(
            src_ref=src, dst_ref=dst, send_sem=s, recv_sem=r, device_id=target, device_id_type=MESH
        )

    out_going = {
        (kind, r): remote(
            send.at[kind, r // 2], take.at[kind, SPOT[r]], d_send.at[kind, r], d_recv.at[kind, r], chip_at(r)
        )
        for r in FAR
        for kind in (0, 1)
    }
    returning = {
        r: remote(part.at[:, SPOT[r]], back_h.at[:, SPOT[r]], r_send.at[r], r_recv.at[r], chip_at(r))
        for r in FAR
    }
    swaps = [
        remote(src, dst, w_send.at[i], w_recv.at[i], twin)
        for i, (src, dst) in enumerate(
            ((wg_h.at[0], twin_w.at[0]), (wu_h.at[0], twin_w.at[1]), (wd_h.at[0], twin_d))
        )
    ]
    teacher_copy = remote(sta_h.at[0], tea.at[0], t_send.at[0], t_recv.at[0], after)
    teacher_swap = remote(tea.at[0], tea.at[1], t_send.at[1], t_recv.at[1], across)

    loads[0].wait()
    loads[1].wait()
    hits, chosen, weight = slot_tables(ids, prob, chip)

    def of_experts(table):
        return jnp.concatenate([table[SPOT[r] * CAP : SPOT[r] * CAP + CAP] for r in (0, 2, 4, 6)], axis=0)

    gather = of_experts(chosen).astype(BF16)
    slot_prob = jnp.sum(of_experts(weight), axis=1, keepdims=True)
    loads[2].wait()
    for n in range(0, 2048, STEP):
        cut = slice(n, n + STEP)
        send[0, :, :, cut] = dot(gather, tok[:, cut]).astype(BF16).reshape(4, CAP, STEP)
    pl.semaphore_wait(barrier, 18)
    teacher_copy.start()
    first_class = FAR[0]
    out_going[0, first_class].start()
    loads[3].wait()
    for n in range(0, 2048, STEP):
        cut = slice(n, n + STEP)
        send[1, :, :, cut] = (slot_prob * dot(gather, cot[:, cut])).astype(BF16).reshape(4, CAP, STEP)
    out_going[1, first_class].start()
    for batch in BATCHES[2:]:
        for kind in (0, 1):
            for r in batch:
                out_going[kind, r].start()
    for copy in swaps:
        copy.start()

    take[:, 0] = send[:, 0]

    mine = (z == 0).astype(jnp.int32)

    def swap_teachers():
        teacher_copy.wait_recv()

        @pl.when(z == 0)
        def _():
            teacher_swap.start()

    teacher_out = pltpu.make_async_copy(tea.at[mine], tea_h, out_sem.at[1])

    def tell():
        loads[4].wait()
        loads[5].wait()

        @pl.when(z == 0)
        def _():
            teacher_swap.wait()

        teacher_out.start()
        student = stu[...].astype(F32)
        teacher = tea[mine].astype(F32)
        eye, label_hit = logit_views(lab, student.shape[1], grp)
        lane = lax.broadcasted_iota(jnp.int32, (8, 128), 1)
        top_s = jnp.max(student, axis=1, keepdims=True)
        top_t = jnp.max(teacher, axis=1, keepdims=True)
        exp_t = jnp.exp(teacher - top_t)
        stats = (
            top_s,
            top_t,
            jnp.sum(jnp.exp(student - top_s), axis=1, keepdims=True),
            jnp.sum(exp_t, axis=1, keepdims=True),
            jnp.sum(exp_t * (teacher - student), axis=1, keepdims=True),
            jnp.sum(jnp.where(label_hit, student, 0.0), axis=1, keepdims=True),
        )
        stat[...] = total([jnp.where(lane == i, s, 0.0) for i, s in enumerate(stats)])
        stat_own.start()
        for copy in telling:
            copy.start()

    stat_own = pltpu.make_async_copy(stat, stat_h.at[0], out_sem.at[2])
    telling = [
        remote(stat, stat_h.at[k], s_send.at[k], s_recv.at[k], member_at(k)) for k in range(1, 16)
    ]
    back_own = pltpu.make_async_copy(part.at[:, 0], back_h.at[:, 0], out_sem.at[0])

    for copy in loads[6:]:
        copy.wait()
    for copy in swaps:
        copy.wait()
    halves = ((wg, wu, wd), (twin_w.at[0], twin_w.at[1], twin_d))
    for step, batch in enumerate(BATCHES):
        for r in batch:
            if r:
                out_going[0, r].wait_recv()
                out_going[1, r].wait_recv()
        first, count = SPOT[batch[0]], len(batch)
        x = take[0, first : first + count].reshape(count * CAP, 2048)
        s = take[1, first : first + count].reshape(count * CAP, 2048)
        inner = []
        for gate_w, up_w, down_w in halves:
            gate = dot_nt(x, gate_w[...])
            up = dot_nt(x, up_w[...])
            grad = dot_nt(s, down_w[...])
            sig = jax.nn.sigmoid(gate)
            hidden = (gate * sig * up).astype(BF16)
            grad_gate = (grad * up * sig * (1.0 + gate * (1.0 - sig))).astype(BF16)
            grad_up = (grad * gate * sig).astype(BF16)
            inner.append((hidden, grad_gate, grad_up))
        for n in range(0, 2048, STEP):
            cut = slice(n, n + STEP)
            out_piece = total([dot(i[0], h[2][:, cut]) for i, h in zip(inner, halves)])
            grad_piece = total(
                [dot(i[1], h[0][:, cut]) + dot(i[2], h[1][:, cut]) for i, h in zip(inner, halves)]
            )
            part[0, first : first + count, :, cut] = out_piece.astype(BF16).reshape(count, CAP, STEP)
            part[1, first : first + count, :, cut] = grad_piece.astype(BF16).reshape(count, CAP, STEP)
        for r in batch:
            if r:
                returning[r].start()
            else:
                back_own.start()
        if step == SWAP_AT:
            swap_teachers()
        if step == TELL_AT:
            tell()

    for copy in (teacher_out, stat_own, back_own):
        copy.wait()
    teacher_copy.wait_send()
    for copy in telling:
        copy.wait()
    for r in FAR:
        for kind in (0, 1):
            out_going[kind, r].wait_send()
        returning[r].wait()


def token_kernel(
    cot_h, ids_h, prob_h, back_h, stu_h, tea_h, lab_h, stat_h,
    lay_h, ing_h, pgr_h, loss_h, lgr_h,
    cot, ids, prob, back, stu, tea, lab, stat, lay, ing, pgr, loss, lgr, in_sem, back_sem, out_sem, row_sem,
):
    grp = lax.axis_index("grp")
    small = [
        pltpu.make_async_copy(src, dst, in_sem.at[i])
        for i, (src, dst) in enumerate(
            (
                (ids_h, ids), (prob_h, prob), (stat_h, stat), (lab_h, lab), (stu_h.at[0], stu), (tea_h, tea),
                (cot_h, cot),
            )
        )
    ]
    cuts = [slice(n, n + STEP) for n in range(0, 2048, STEP)]
    big = [
        pltpu.make_async_copy(back_h.at[:, :, :, cut], back.at[:, :, :, cut], back_sem.at[i])
        for i, cut in enumerate(cuts)
    ]
    for copy in small + big:
        copy.start()
    stores = [
        pltpu.make_async_copy(src, dst, out_sem.at[i])
        for i, (src, dst) in enumerate(((pgr, pgr_h), (loss, loss_h), (lgr, lgr_h.at[0])))
    ]

    small[0].wait()
    small[1].wait()
    hits, chosen, weight = slot_tables(ids, prob, grp // 2)
    weight_t = weight.T
    chosen_t = chosen.T.astype(BF16)
    weight_hi = weight_t.astype(BF16)
    weight_lo = (weight_t - weight_hi.astype(F32)).astype(BF16)
    for copy in small[2:6]:
        copy.wait()
    seen = [stat[k] for k in range(16)]

    def col(k, i):
        return seen[k][:, i : i + 1]

    max_s = functools.reduce(jnp.maximum, [col(k, 0) for k in range(16)])
    max_t = functools.reduce(jnp.maximum, [col(k, 1) for k in range(16)])
    scale_s = [jnp.exp(col(k, 0) - max_s) for k in range(16)]
    scale_t = [jnp.exp(col(k, 1) - max_t) for k in range(16)]
    sum_s = total([col(k, 2) * scale_s[k] for k in range(16)])
    sum_t = total([col(k, 3) * scale_t[k] for k in range(16)])
    cross = total([col(k, 4) * scale_t[k] for k in range(16)])
    label_logit = total([col(k, 5) for k in range(16)])
    lse_s = max_s + jnp.log(sum_s)
    lse_t = max_t + jnp.log(sum_t)
    student = stu[...].astype(F32)
    teacher = tea[...].astype(F32)
    eye, label_hit = logit_views(lab, student.shape[1], grp)
    value = 2.0 * lse_s - label_logit + cross / sum_t - lse_t
    loss[...] = jnp.sum(jnp.where(eye, value, 0.0), axis=0, keepdims=True)
    onehot = jnp.where(label_hit, 1.0, 0.0)
    lgr[...] = (2.0 * jnp.exp(student - lse_s) - onehot - jnp.exp(teacher - lse_t)).astype(BF16)
    stores[1].start()
    stores[2].start()

    small[6].wait()
    inner_product = jnp.zeros((CHIPS * CAP, 128), F32)
    row_stores = []
    for i, cut in enumerate(cuts):
        big[i].wait()
        rows = back[0, :, :, cut].reshape(CHIPS * CAP, STEP)
        lay[:, cut] = (dot(weight_hi, rows) + dot(weight_lo, rows)).astype(BF16)
        ing[:, cut] = dot(chosen_t, back[1, :, :, cut].reshape(CHIPS * CAP, STEP)).astype(BF16)
        for j, (src, dst) in enumerate(((lay, lay_h), (ing, ing_h))):
            copy = pltpu.make_async_copy(src.at[:, cut], dst.at[:, cut], row_sem.at[j, i])
            copy.start()
            row_stores.append(copy)
        inner_product = inner_product + dot_nt(rows, cot[:, cut])
    inner_product = inner_product * chosen
    for k, h in enumerate(hits):
        pgr[k : k + 1, :] = jnp.sum(jnp.where(h, inner_product, 0.0), axis=0, keepdims=True)
    stores[0].start()
    for copy in stores + row_stores:
        copy.wait()


def body(tokens, cotangent, expert_ids, route_prob, w_gate, w_up, w_down, student, stale, labels):
    expert_ids, route_prob = expert_ids.T, route_prob.T
    w_gate, w_up = jnp.swapaxes(w_gate, 1, 2), jnp.swapaxes(w_up, 1, 2)
    width = student.shape[2]
    logits = (8, width)
    blocks = (2, CHIPS, CAP, 2048)
    dma = pltpu.SemaphoreType.DMA
    anywhere = pl.BlockSpec(memory_space=pl.ANY)
    back, stats, teacher = pl.pallas_call(
        expert_kernel,
        name="experts",
        out_shape=(
            jax.ShapeDtypeStruct(blocks, BF16),
            jax.ShapeDtypeStruct((16, 8, 128), F32),
            jax.ShapeDtypeStruct(logits, BF16),
        ),
        in_specs=[anywhere] * 10,
        out_specs=[anywhere] * 3,
        scratch_shapes=[
            pltpu.VMEM(tokens.shape, BF16),
            pltpu.VMEM(tokens.shape, BF16),
            pltpu.VMEM(expert_ids.shape, jnp.int32),
            pltpu.VMEM(route_prob.shape, F32),
            pltpu.VMEM(w_gate.shape[1:], BF16),
            pltpu.VMEM(w_up.shape[1:], BF16),
            pltpu.VMEM(w_down.shape[1:], BF16),
            pltpu.VMEM(logits, BF16),
            pltpu.VMEM((2,) + logits, BF16),
            pltpu.VMEM(labels.shape, jnp.int32),
            pltpu.VMEM((2, 4, CAP, 2048), BF16),
            pltpu.VMEM(blocks, BF16),
            pltpu.VMEM(blocks, BF16),
            pltpu.VMEM((8, 128), F32),
            pltpu.VMEM((2,) + w_gate.shape[1:], BF16),
            pltpu.VMEM(w_down.shape[1:], BF16),
            dma((9,)),
            dma((3,)),
            dma((3,)),
            dma((3,)),
            dma((2, 8)),
            dma((2, 8)),
            dma((8,)),
            dma((8,)),
            dma((16,)),
            dma((16,)),
            dma((2,)),
            dma((2,)),
        ],
        compiler_params=pltpu.CompilerParams(
            collective_id=0, has_side_effects=True, vmem_limit_bytes=56 << 20
        ),
    )(tokens, cotangent, expert_ids, route_prob, w_gate, w_up, w_down, student, stale, labels)
    layer_out, input_grad, prob_grad, loss, logit_grad = pl.pallas_call(
        token_kernel,
        name="tokens",
        out_shape=(
            jax.ShapeDtypeStruct(tokens.shape, BF16),
            jax.ShapeDtypeStruct(tokens.shape, BF16),
            jax.ShapeDtypeStruct(route_prob.shape, F32),
            jax.ShapeDtypeStruct(labels.shape, F32),
            jax.ShapeDtypeStruct(student.shape, BF16),
        ),
        in_specs=[anywhere] * 8,
        out_specs=[anywhere] * 5,
        scratch_shapes=[
            pltpu.VMEM(tokens.shape, BF16),
            pltpu.VMEM(expert_ids.shape, jnp.int32),
            pltpu.VMEM(route_prob.shape, F32),
            pltpu.VMEM(blocks, BF16),
            pltpu.VMEM(logits, BF16),
            pltpu.VMEM(logits, BF16),
            pltpu.VMEM(labels.shape, jnp.int32),
            pltpu.VMEM((16, 8, 128), F32),
            pltpu.VMEM(tokens.shape, BF16),
            pltpu.VMEM(tokens.shape, BF16),
            pltpu.VMEM(route_prob.shape, F32),
            pltpu.VMEM(labels.shape, F32),
            pltpu.VMEM(logits, BF16),
            dma((7,)),
            dma((4,)),
            dma((3,)),
            dma((2, 4)),
        ],
        compiler_params=pltpu.CompilerParams(vmem_limit_bytes=56 << 20),
    )(cotangent, expert_ids, route_prob, back, student, teacher, labels, stats)
    return layer_out, input_grad, prob_grad.T, loss, logit_grad


def solution(mesh):
    rows = P(("peer", "grp"), None)
    vocab = P("peer", None, "grp")
    peer_row = P("peer", None)
    return jax.shard_map(
        body,
        mesh=mesh,
        in_specs=(
            rows, rows, rows, rows, vocab, vocab, P("peer", "grp", None), vocab, vocab, peer_row,
        ),
        out_specs=(rows, rows, rows, peer_row, vocab),
        check_vma=False,
    )
```

time: 82.8 us -> 70.2 us (0.85)
  local copies, waits for them, and re-layouts: 11.1 us -> 0 us
  Pallas kernels: 70.8 us -> 69.4 us
    unnamed x18 -> x0, local copies, waits for them, and re-layouts: 9.65 us -> none
    pallas_call x1 -> x0, local copies, waits for them, and re-layouts: 1.49 us -> none  [body(): pl.pallas_call(kernel, name='layer', out_shape=(jax.ShapeDtypeStruct(toke...]
    pallas_call x1 -> x2, Pallas kernels: 70.8 us -> 69.4 us  [the longest x1 65.3 us: body(): pl.pallas_call(expert_kernel, name='experts', out_shape=(jax.ShapeDtypeSt...]
where the time goes in v2:
time: 70.2 us; the launch traced here: 70.1 us
  Pallas kernels  69.4 us (99%)
    pallas_call x1, Pallas kernels, body(): pl.pallas_call(expert_kernel, name='experts', out_shape=(jax.ShapeDtypeSt...  65.3 us
    pallas_call x1, Pallas kernels, body(): pl.pallas_call(token_kernel, name='tokens', out_shape=(jax.ShapeDtypeStru...  4.07 us

profile of v2, /device:TPU:1, one launch (start us, length us, event | category | flops | bytes accessed | tf_op | source)
XLA Modules:
  0.0 70.1 jit_solution(8819611413768337950)
XLA Ops:
  0.6 65.3 %experts.1 = (bf16[2,8,32,2048]{3,2,1,0:T(8,128)(2,1)}, f32[16,8,128]{2,1,0:T(8,128)}, bf16[8,9496]{1,0:T(8,128)(2,1)}) custom-call(bf16[128,2048]{1,0:T(8,128)(2,1)} %tok_h.1, bf16[128,2048]{1,0:T(8,128)(2,1)} %cot_h.3, s32[4,128]{1,0:T(4,128)} %bitcast.7, f32[4,128]{1,0:T(4,128)} %bitcast.9, bf16[1,176,2048]{2,1,0:T(8,128)(2,1)} %bitcast.5, ...), custom_call_target="tpu_custom_call" | custom-call | tf_op jit(solution)/shard_map/experts/pallas_call | solution.py:353
  66.0 4.1 %tokens.1 = (bf16[128,2048]{1,0:T(8,128)(2,1)}, bf16[128,2048]{1,0:T(8,128)(2,1)}, f32[4,128]{1,0:T(4,128)}, f32[1,8]{1,0:T(1,128)}, bf16[1,8,9496]{2,1,0:T(8,128)(2,1)}) custom-call(bf16[128,2048]{1,0:T(8,128)(2,1)} %cot_h.3, s32[4,128]{1,0:T(4,128)} %bitcast.8, f32[4,128]{1,0:T(4,128)} %bitcast.10, bf16[2,8,32,2048]{3,2,1,0:T(8,128)(2,1)} %get-tuple-element.13.back_h, ...), custom_call_target="tpu_custom_call" | custom-call | tf_op jit(solution)/shard_map/tokens/pallas_call | solution.py:397

commit v3 on v2

v3 whole, which is shorter than its diff:
```python
import functools

import jax
import jax.numpy as jnp
from jax import lax
from jax.experimental import pallas as pl
from jax.experimental.pallas import tpu as pltpu
from jax.sharding import PartitionSpec as P

MESH = pl.DeviceIdType.MESH
CAP = 32
EXPERTS = 4
NEAR = (0, 3, 4, 7)
MATE = 1
ORDER = tuple(r for near in NEAR for r in (near, near ^ MATE))
SPOT = {r: i for i, r in enumerate(ORDER)}
KINDS = (0, 1)
STEP = 512
F32 = jnp.float32
BF16 = jnp.bfloat16
NT = (((1,), (1,)), ((), ()))


def dot(a, b):
    return jnp.dot(a, b, preferred_element_type=F32)


def dot_nt(a, b):
    return lax.dot_general(a, b, NT, preferred_element_type=F32)


def total(terms):
    return functools.reduce(jnp.add, terms)


def xor(a, bits, width):
    out = a
    for b in range(width):
        if bits >> b & 1:
            out = out + (1 << b) * (1 - 2 * ((a // (1 << b)) % 2))
    return out


def row_experts(chip):
    rows = lax.broadcasted_iota(jnp.int32, (EXPERTS * CAP, 128), 0)
    return total([jnp.where(rows // CAP == j, xor(chip // 2, j, 2), 0) for j in range(EXPERTS)])


def slot_tables(ids, prob, chip):
    rows = lax.broadcasted_iota(jnp.int32, (EXPERTS * CAP, 128), 0)
    row_expert = row_experts(chip)
    hits = [ids[k : k + 1, :] == row_expert for k in range(4)]
    member = total([h.astype(F32) for h in hits])
    earlier = (
        lax.broadcasted_iota(jnp.int32, (128, 128), 0) < lax.broadcasted_iota(jnp.int32, (128, 128), 1)
    )
    position = dot(member.astype(BF16), earlier.astype(F32).astype(BF16))
    chosen = jnp.where((member > 0.0) & (position.astype(jnp.int32) == rows % CAP), 1.0, 0.0)
    weight = total([jnp.where(h, prob[k : k + 1, :], 0.0) for k, h in enumerate(hits)]) * chosen
    return chosen, weight


def logit_views(lab, width, grp):
    eye = lax.broadcasted_iota(jnp.int32, (8, 8), 0) == lax.broadcasted_iota(jnp.int32, (8, 8), 1)
    label = jnp.sum(jnp.where(eye, lab[...].astype(F32), 0.0), axis=1, keepdims=True).astype(jnp.int32)
    vocab = grp * width + lax.broadcasted_iota(jnp.int32, (8, width), 1)
    return eye, vocab == label


def expert_kernel(
    tok_h, cot_h, ids_h, prob_h, wg_h, wu_h, wd_h, stu_h, sta_h, lab_h,
    back_h, table_h, loss_h, lgr_h,
    tok, cot, ids, prob, wg, wu, wd, stu, tea, lab, send, take, own, part, mate, whole, told, heard, table, loss, lgr, twin_w, twin_d,
    in_sem, out_sem, w_send, w_recv, d_send, d_recv, m_send, m_recv, r_send, r_recv, s_send, s_recv, t_send, t_recv,
):
    peer, grp = lax.axis_index("peer"), lax.axis_index("grp")
    n_peer = lax.axis_size("peer")
    chip, core = grp // 2, grp % 2
    twin = (peer, chip * 2 + (1 - core))
    depth = n_peer // 2
    half, z = peer // depth, lax.rem(peer, depth)
    after = (half * depth + lax.rem(z + 1, depth), grp)
    before = (half * depth + lax.rem(z + depth - 1, depth), grp)
    across = ((1 - half) * depth + z, grp)

    def chip_at(r):
        return (peer, xor(chip, r, 3) * 2 + core)

    barrier = pltpu.get_barrier_semaphore()
    partners = (twin,) + tuple(chip_at(r) for r in (MATE,) + NEAR[1:]) + (after, before, across)
    for partner in partners:
        pl.semaphore_signal(barrier, inc=1, device_id=partner, device_id_type=MESH)

    loads = [
        pltpu.make_async_copy(src, dst, in_sem.at[i])
        for i, (src, dst) in enumerate(
            (
                (ids_h, ids), (prob_h, prob), (tok_h, tok), (cot_h, cot), (stu_h.at[0], stu), (lab_h, lab),
                (wg_h.at[0], wg), (wu_h.at[0], wu), (wd_h.at[0], wd),
            )
        )
    ]
    for copy in loads[:4]:
        copy.start()

    def remote(src, dst, s, r, target):
        return pltpu.make_async_remote_copy(
            src_ref=src, dst_ref=dst, send_sem=s, recv_sem=r, device_id=target, device_id_type=MESH
        )

    def block_to(r, kind, source, target):
        return remote(source, take.at[kind, SPOT[r]], d_send.at[kind, r], d_recv.at[kind, r], chip_at(target))

    out_going = {
        (kind, r): block_to(r, kind, send.at[kind, r // 2], r) for r in (MATE,) + NEAR[1:] for kind in KINDS
    }
    handed_on = {
        (kind, r): block_to(r ^ MATE, kind, take.at[kind, SPOT[r]], MATE) for r in NEAR[1:] for kind in KINDS
    }
    partial = {
        (kind, j): remote(
            part.at[kind, j], mate.at[kind, j], m_send.at[kind, j], m_recv.at[kind, j], chip_at(MATE)
        )
        for j in range(EXPERTS)
        for kind in KINDS
    }
    returning = {
        (kind, j): remote(
            whole.at[kind, j], back_h.at[kind, j], r_send.at[kind, j], r_recv.at[kind, j], chip_at(NEAR[j])
        )
        for j in range(1, EXPERTS)
        for kind in KINDS
    }
    swaps = [
        remote(src, dst, w_send.at[i], w_recv.at[i], twin)
        for i, (src, dst) in enumerate(
            ((wg_h.at[0], twin_w.at[0]), (wu_h.at[0], twin_w.at[1]), (wd_h.at[0], twin_d))
        )
    ]
    teacher_copy = remote(sta_h.at[0], tea.at[0], t_send.at[0], t_recv.at[0], after)
    teacher_swap = remote(tea.at[0], tea.at[1], t_send.at[1], t_recv.at[1], across)

    loads[0].wait()
    loads[1].wait()
    chosen, weight = slot_tables(ids, prob, chip)

    gather = chosen.astype(BF16)
    slot_prob = jnp.sum(weight, axis=1, keepdims=True)
    loads[2].wait()
    for n in range(0, 2048, STEP):
        cut = slice(n, n + STEP)
        send[0, :, :, cut] = dot(gather, tok[:, cut]).astype(BF16).reshape(EXPERTS, CAP, STEP)
    pl.semaphore_wait(barrier, len(partners))
    teacher_copy.start()
    for r in (MATE, 3, 4):
        out_going[0, r].start()
    for copy in loads[4:]:
        copy.start()
    loads[3].wait()
    for n in range(0, 2048, STEP):
        cut = slice(n, n + STEP)
        send[1, :, :, cut] = (slot_prob * dot(gather, cot[:, cut])).astype(BF16).reshape(EXPERTS, CAP, STEP)
    for r in (MATE, 3, 4):
        out_going[1, r].start()
    for kind in KINDS:
        out_going[kind, 7].start()
    for copy in swaps:
        copy.start()

    take[:, 0] = send[:, 0]

    def hand_on(r):
        for kind in KINDS:
            out_going[kind, r].wait_recv()
            handed_on[kind, r].start()

    mine = (z == 0).astype(jnp.int32)

    def swap_teachers():
        teacher_copy.wait_recv()

        @pl.when(z == 0)
        def _():
            teacher_swap.start()

    def local_stats():
        loads[4].wait()
        loads[5].wait()

        @pl.when(z == 0)
        def _():
            teacher_swap.wait()

        student = stu[...].astype(F32)
        teacher = tea[mine].astype(F32)
        label_hit = logit_views(lab, student.shape[1], grp)[1]
        top_s = jnp.max(student, axis=1, keepdims=True)
        top_t = jnp.max(teacher, axis=1, keepdims=True)
        exp_t = jnp.exp(teacher - top_t)
        return (
            top_s,
            top_t,
            jnp.sum(jnp.exp(student - top_s), axis=1, keepdims=True),
            jnp.sum(exp_t, axis=1, keepdims=True),
            jnp.sum(exp_t * (teacher - student), axis=1, keepdims=True),
            jnp.sum(jnp.where(label_hit, student, 0.0), axis=1, keepdims=True),
        )

    telling = [
        remote(told.at[i], heard.at[i], s_send.at[i], s_recv.at[i], target)
        for i, target in enumerate((twin, chip_at(MATE), chip_at(3), chip_at(4)))
    ]

    def tell(i, stats):
        lane = lax.broadcasted_iota(jnp.int32, (8, 128), 1)
        told[i] = total([jnp.where(lane == k, v, 0.0) for k, v in enumerate(stats)])
        telling[i].start()

    def join(i, stats):
        telling[i].wait_recv()
        other = [heard[i, :, k : k + 1] for k in range(6)]
        tops = [jnp.maximum(a, b) for a, b in zip(stats[:2], other[:2])]
        scales = [
            (jnp.exp(a - top), jnp.exp(b - top)) for a, b, top in zip(stats[:2], other[:2], tops)
        ]
        sums = [
            stats[k] * scales[m][0] + other[k] * scales[m][1] for k, m in ((2, 0), (3, 1), (4, 1))
        ]
        return (*tops, *sums, stats[5] + other[5])

    def finish_loss(stats):
        top_s, top_t, sum_s, sum_t, cross, label_logit = stats
        lse_s = top_s + jnp.log(sum_s)
        lse_t = top_t + jnp.log(sum_t)
        student = stu[...].astype(F32)
        teacher = tea[mine].astype(F32)
        eye, label_hit = logit_views(lab, student.shape[1], grp)
        value = 2.0 * lse_s - label_logit + cross / sum_t - lse_t
        loss[...] = jnp.sum(jnp.where(eye, value, 0.0), axis=0, keepdims=True)
        onehot = jnp.where(label_hit, 1.0, 0.0)
        lgr[...] = (2.0 * jnp.exp(student - lse_s) - onehot - jnp.exp(teacher - lse_t)).astype(BF16)

    stores = [
        pltpu.make_async_copy(src, dst, out_sem.at[i])
        for i, (src, dst) in enumerate(
            ((whole.at[:, 0], back_h.at[:, 0]), (table, table_h), (loss, loss_h), (lgr, lgr_h.at[0]))
        )
    ]

    hand_on(3)
    hand_on(4)

    for copy in loads[6:]:
        copy.wait()
    for copy in swaps:
        copy.wait()
    halves = ((wg, wu, wd), (twin_w.at[0], twin_w.at[1], twin_d))

    def work(j):
        spots = slice(2 * j, 2 * j + 2)
        x = take[0, spots].reshape(2 * CAP, 2048)
        s = take[1, spots].reshape(2 * CAP, 2048)
        inner = []
        for gate_w, up_w, down_w in halves:
            gate = dot_nt(x, gate_w[...])
            up = dot_nt(x, up_w[...])
            grad = dot_nt(s, down_w[...])
            sig = jax.nn.sigmoid(gate)
            hidden = (gate * sig * up).astype(BF16)
            grad_gate = (grad * up * sig * (1.0 + gate * (1.0 - sig))).astype(BF16)
            grad_up = (grad * gate * sig).astype(BF16)
            inner.append((hidden, grad_gate, grad_up))
        for n in range(0, 2048, STEP):
            cut = slice(n, n + STEP)
            pieces = (
                total([dot(i[0], h[2][:, cut]) for i, h in zip(inner, halves)]),
                total([dot(i[1], h[0][:, cut]) + dot(i[2], h[1][:, cut]) for i, h in zip(inner, halves)]),
            )
            for kind, piece in enumerate(pieces):
                own[kind, j, :, cut] = piece[:CAP]
                part[kind, j, :, cut] = piece[CAP:].astype(BF16)

    def wait_block(r):
        for kind in KINDS:
            (handed_on[kind, r ^ MATE] if (kind, r ^ MATE) in handed_on else out_going[kind, r]).wait_recv()

    wait_block(MATE)
    work(0)
    swap_teachers()
    hand_on(7)
    wait_block(2)
    work(1)
    for kind in KINDS:
        partial[kind, 1].start()
    stats = local_stats()
    tell(0, stats)
    wait_block(5)
    work(2)
    for kind in KINDS:
        partial[kind, 2].start()
    stats = join(0, stats)
    tell(1, stats)
    wait_block(6)
    work(3)
    for j in (3, 0):
        for kind in KINDS:
            partial[kind, j].start()
    weight_t = weight.T
    weight_hi = weight_t.astype(BF16)
    table[0] = weight_hi
    table[1] = (weight_t - weight_hi.astype(F32)).astype(BF16)
    table[2] = chosen.T.astype(BF16)
    table[3] = gather
    stores[1].start()

    def add_up(j):
        for kind in KINDS:
            partial[kind, j].wait_recv()
            whole[kind, j] = (own[kind, j] + mate[kind, j].astype(F32)).astype(BF16)
            if j:
                returning[kind, j].start()

    add_up(1)
    stats = join(1, stats)
    tell(2, stats)
    add_up(2)
    stats = join(2, stats)
    tell(3, stats)
    add_up(3)
    finish_loss(join(3, stats))
    stores[2].start()
    stores[3].start()
    add_up(0)
    stores[0].start()

    teacher_copy.wait_send()
    for copy in telling:
        copy.wait_send()
    for copies in (out_going, handed_on, partial):
        for copy in copies.values():
            copy.wait_send()
    for copy in returning.values():
        copy.wait()
    for copy in stores:
        copy.wait()


def token_kernel(
    cot_h, ids_h, back_h, table_h, losses_h, logits_h,
    lay_h, ing_h, pgr_h, loss_h, lgr_h,
    cot, ids, back, table, loss, lgr, lay, ing, pgr, in_sem, back_sem, out_sem, row_sem,
):
    grp = lax.axis_index("grp")
    cuts = [slice(n, n + STEP) for n in range(0, 2048, STEP)]
    small = [
        pltpu.make_async_copy(src, dst, in_sem.at[i])
        for i, (src, dst) in enumerate(
            ((table_h, table), (ids_h, ids), (losses_h, loss), (logits_h.at[0], lgr))
        )
    ]
    big = [
        (
            pltpu.make_async_copy(back_h.at[:, :, :, cut], back.at[:, :, :, cut], back_sem.at[0, i]),
            pltpu.make_async_copy(cot_h.at[:, cut], cot.at[:, cut], back_sem.at[1, i]),
        )
        for i, cut in enumerate(cuts)
    ]
    handed = [
        pltpu.make_async_copy(src, dst, out_sem.at[i])
        for i, (src, dst) in enumerate(((loss, loss_h), (lgr, lgr_h.at[0])))
    ]
    store = pltpu.make_async_copy(pgr, pgr_h, out_sem.at[2])
    for copy in small[:2]:
        copy.start()
    for pair in big:
        for copy in pair:
            copy.start()
    for copy in small[2:]:
        copy.start()
    for copy in small[:2]:
        copy.wait()
    inner_product = jnp.zeros((EXPERTS * CAP, 128), F32)
    row_stores = []
    for i, cut in enumerate(cuts):
        for copy in big[i]:
            copy.wait()
        rows = back[0, :, :, cut].reshape(EXPERTS * CAP, STEP)
        lay[:, cut] = (dot(table[0], rows) + dot(table[1], rows)).astype(BF16)
        ing[:, cut] = dot(table[2], back[1, :, :, cut].reshape(EXPERTS * CAP, STEP)).astype(BF16)
        for j, (src, dst) in enumerate(((lay, lay_h), (ing, ing_h))):
            copy = pltpu.make_async_copy(src.at[:, cut], dst.at[:, cut], row_sem.at[j, i])
            copy.start()
            row_stores.append(copy)
        inner_product = inner_product + dot_nt(rows, cot[:, cut])
    for arrived, copy in zip(small[2:], handed):
        arrived.wait()
        copy.start()
    inner_product = inner_product * table[3].astype(F32)
    expert = row_experts(grp // 2)
    for k in range(4):
        pgr[k : k + 1, :] = jnp.sum(
            jnp.where(ids[k : k + 1, :] == expert, inner_product, 0.0), axis=0, keepdims=True
        )
    store.start()
    for copy in handed + row_stores + [store]:
        copy.wait()


def body(tokens, cotangent, expert_ids, route_prob, w_gate, w_up, w_down, student, stale, labels):
    expert_ids, route_prob = expert_ids.T, route_prob.T
    w_gate, w_up = jnp.swapaxes(w_gate, 1, 2), jnp.swapaxes(w_up, 1, 2)
    width = student.shape[2]
    logits = (8, width)
    blocks = (2, EXPERTS, CAP, 2048)
    tables = (4, 128, EXPERTS * CAP)
    dma = pltpu.SemaphoreType.DMA
    anywhere = pl.BlockSpec(memory_space=pl.ANY)
    back, table, losses, logit_rows = pl.pallas_call(
        expert_kernel,
        name="experts",
        out_shape=(
            jax.ShapeDtypeStruct(blocks, BF16),
            jax.ShapeDtypeStruct(tables, BF16),
            jax.ShapeDtypeStruct(labels.shape, F32),
            jax.ShapeDtypeStruct(student.shape, BF16),
        ),
        in_specs=[anywhere] * 10,
        out_specs=[anywhere] * 4,
        scratch_shapes=[
            pltpu.VMEM(tokens.shape, BF16),
            pltpu.VMEM(tokens.shape, BF16),
            pltpu.VMEM(expert_ids.shape, jnp.int32),
            pltpu.VMEM(route_prob.shape, F32),
            pltpu.VMEM(w_gate.shape[1:], BF16),
            pltpu.VMEM(w_up.shape[1:], BF16),
            pltpu.VMEM(w_down.shape[1:], BF16),
            pltpu.VMEM(logits, BF16),
            pltpu.VMEM((2,) + logits, BF16),
            pltpu.VMEM(labels.shape, jnp.int32),
            pltpu.VMEM(blocks, BF16),
            pltpu.VMEM((2, 2 * EXPERTS, CAP, 2048), BF16),
            pltpu.VMEM(blocks, F32),
            pltpu.VMEM(blocks, BF16),
            pltpu.VMEM(blocks, BF16),
            pltpu.VMEM(blocks, BF16),
            pltpu.VMEM((4, 8, 128), F32),
            pltpu.VMEM((4, 8, 128), F32),
            pltpu.VMEM(tables, BF16),
            pltpu.VMEM(labels.shape, F32),
            pltpu.VMEM(logits, BF16),
            pltpu.VMEM((2,) + w_gate.shape[1:], BF16),
            pltpu.VMEM(w_down.shape[1:], BF16),
            dma((9,)),
            dma((4,)),
            dma((3,)),
            dma((3,)),
            dma((2, 8)),
            dma((2, 8)),
            dma((2, EXPERTS)),
            dma((2, EXPERTS)),
            dma((2, EXPERTS)),
            dma((2, EXPERTS)),
            dma((4,)),
            dma((4,)),
            dma((2,)),
            dma((2,)),
        ],
        compiler_params=pltpu.CompilerParams(
            collective_id=0, has_side_effects=True, vmem_limit_bytes=56 << 20
        ),
    )(tokens, cotangent, expert_ids, route_prob, w_gate, w_up, w_down, student, stale, labels)
    layer_out, input_grad, prob_grad, loss, logit_grad = pl.pallas_call(
        token_kernel,
        name="tokens",
        out_shape=(
            jax.ShapeDtypeStruct(tokens.shape, BF16),
            jax.ShapeDtypeStruct(tokens.shape, BF16),
            jax.ShapeDtypeStruct(route_prob.shape, F32),
            jax.ShapeDtypeStruct(labels.shape, F32),
            jax.ShapeDtypeStruct(student.shape, BF16),
        ),
        in_specs=[anywhere] * 6,
        out_specs=[anywhere] * 5,
        scratch_shapes=[
            pltpu.VMEM(tokens.shape, BF16),
            pltpu.VMEM(expert_ids.shape, jnp.int32),
            pltpu.VMEM(blocks, BF16),
            pltpu.VMEM(tables, BF16),
            pltpu.VMEM(labels.shape, F32),
            pltpu.VMEM(logits, BF16),
            pltpu.VMEM(tokens.shape, BF16),
            pltpu.VMEM(tokens.shape, BF16),
            pltpu.VMEM(route_prob.shape, F32),
            dma((4,)),
            dma((2, 4)),
            dma((3,)),
            dma((2, 4)),
        ],
        compiler_params=pltpu.CompilerParams(vmem_limit_bytes=56 << 20),
    )(cotangent, expert_ids, back, table, losses, logit_rows)
    return layer_out, input_grad, prob_grad.T, loss, logit_grad


def solution(mesh):
    rows = P(("peer", "grp"), None)
    vocab = P("peer", None, "grp")
    peer_row = P("peer", None)
    return jax.shard_map(
        body,
        mesh=mesh,
        in_specs=(
            rows, rows, rows, rows, vocab, vocab, P("peer", "grp", None), vocab, vocab, peer_row,
        ),
        out_specs=(rows, rows, rows, peer_row, vocab),
        check_vma=False,
    )
```

time: 70.2 us -> 67.1 us (0.956)
  the two profiles are of different devices: /device:TPU:1 before, /device:TPU:2 now
where the time goes in v3:
time: 67.1 us; the launch traced here: 66.9 us
  Pallas kernels  66.3 us (99%)
    pallas_call x1, Pallas kernels, body(): pl.pallas_call(expert_kernel, name='experts', out_shape=(jax.ShapeDtypeSt...  62.9 us
    pallas_call x1, Pallas kernels, body(): pl.pallas_call(token_kernel, name='tokens', out_shape=(jax.ShapeDtypeStru...  3.32 us

profile of v3, /device:TPU:2, one launch (start us, length us, event | category | flops | bytes accessed | tf_op | source)
XLA Modules:
  0.0 66.9 jit_solution(11674533973392158195)
XLA Ops:
  0.6 62.9 %experts.1 = (bf16[2,4,32,2048]{3,2,1,0:T(8,128)(2,1)}, bf16[4,128,128]{2,1,0:T(8,128)(2,1)}, f32[1,8]{1,0:T(1,128)}, bf16[1,8,9496]{2,1,0:T(8,128)(2,1)}) custom-call(bf16[128,2048]{1,0:T(8,128)(2,1)} %tok_h.1, bf16[128,2048]{1,0:T(8,128)(2,1)} %cot_h.3, s32[4,128]{1,0:T(4,128)} %bitcast.7, f32[4,128]{1,0:T(4,128)} %bitcast.9, ...), custom_call_target="tpu_custom_call" | custom-call | tf_op jit(solution)/shard_map/experts/pallas_call | solution.py:418
  63.6 3.3 %tokens.1 = (bf16[128,2048]{1,0:T(8,128)(2,1)}, bf16[128,2048]{1,0:T(8,128)(2,1)}, f32[4,128]{1,0:T(4,128)}, f32[1,8]{1,0:T(1,128)}, bf16[1,8,9496]{2,1,0:T(8,128)(2,1)}) custom-call(bf16[128,2048]{1,0:T(8,128)(2,1)} %cot_h.3, s32[4,128]{1,0:T(4,128)} %bitcast.8, bf16[2,4,32,2048]{3,2,1,0:T(8,128)(2,1)} %get-tuple-element.14.back_h, ...), custom_call_target="tpu_custom_call" | custom-call | tf_op jit(solution)/shard_map/tokens/pallas_call | solution.py:472

commit v4 on v3

--- a/solution.py
+++ b/solution.py
@@ -108,6 +108,9 @@
             src_ref=src, dst_ref=dst, send_sem=s, recv_sem=r, device_id=target, device_id_type=MESH
         )
 
+    def both_to(r, source, target):
+        return remote(source, take.at[:, SPOT[r]], d_send.at[0, r], d_recv.at[0, r], chip_at(target))
+
     def block_to(r, kind, source, target):
         return remote(source, take.at[kind, SPOT[r]], d_send.at[kind, r], d_recv.at[kind, r], chip_at(target))
 
@@ -115,15 +118,19 @@
         (kind, r): block_to(r, kind, send.at[kind, r // 2], r) for r in (MATE,) + NEAR[1:] for kind in KINDS
     }
     handed_on = {
-        (kind, r): block_to(r ^ MATE, kind, take.at[kind, SPOT[r]], MATE) for r in NEAR[1:] for kind in KINDS
+        (kind, r): block_to(r ^ MATE, kind, take.at[kind, SPOT[r]], MATE) for r in (3,) for kind in KINDS
     }
+    for r in NEAR[2:]:
+        handed_on[0, r] = both_to(r ^ MATE, take.at[:, SPOT[r]], MATE)
     partial = {
         (kind, j): remote(
             part.at[kind, j], mate.at[kind, j], m_send.at[kind, j], m_recv.at[kind, j], chip_at(MATE)
         )
-        for j in range(EXPERTS)
+        for j in (0, 3)
         for kind in KINDS
     }
+    for j in (1, 2):
+        partial[0, j] = remote(part.at[:, j], mate.at[:, j], m_send.at[0, j], m_recv.at[0, j], chip_at(MATE))
     returning = {
         (kind, j): remote(
             whole.at[kind, j], back_h.at[kind, j], r_send.at[kind, j], r_recv.at[kind, j], chip_at(NEAR[j])
@@ -172,7 +179,10 @@
     def hand_on(r):
         for kind in KINDS:
             out_going[kind, r].wait_recv()
-            handed_on[kind, r].start()
+            if (1, r) in handed_on:
+                handed_on[kind, r].start()
+        if (1, r) not in handed_on:
+            handed_on[0, r].start()
 
     mine = (z == 0).astype(jnp.int32)
 
@@ -243,7 +253,10 @@
     stores = [
         pltpu.make_async_copy(src, dst, out_sem.at[i])
         for i, (src, dst) in enumerate(
-            ((whole.at[:, 0], back_h.at[:, 0]), (table, table_h), (loss, loss_h), (lgr, lgr_h.at[0]))
+            (
+                (whole.at[0, 0], back_h.at[0, 0]), (table, table_h), (loss, loss_h), (lgr, lgr_h.at[0]),
+                (whole.at[1, 0], back_h.at[1, 0]),
+            )
         )
     ]
 
@@ -281,8 +294,10 @@
                 part[kind, j, :, cut] = piece[CAP:].astype(BF16)
 
     def wait_block(r):
-        for kind in KINDS:
-            (handed_on[kind, r ^ MATE] if (kind, r ^ MATE) in handed_on else out_going[kind, r]).wait_recv()
+        for copies, key in ((handed_on, r ^ MATE), (out_going, r)):
+            for kind in KINDS:
+                if (kind, key) in copies:
+                    copies[kind, key].wait_recv()
 
     wait_block(MATE)
     work(0)
@@ -290,14 +305,12 @@
     hand_on(7)
     wait_block(2)
     work(1)
-    for kind in KINDS:
-        partial[kind, 1].start()
+    partial[0, 1].start()
     stats = local_stats()
     tell(0, stats)
     wait_block(5)
     work(2)
-    for kind in KINDS:
-        partial[kind, 2].start()
+    partial[0, 2].start()
     stats = join(0, stats)
     tell(1, stats)
     wait_block(6)
@@ -315,10 +328,13 @@
 
     def add_up(j):
         for kind in KINDS:
-            partial[kind, j].wait_recv()
+            if (kind, j) in partial:
+                partial[kind, j].wait_recv()
             whole[kind, j] = (own[kind, j] + mate[kind, j].astype(F32)).astype(BF16)
             if j:
                 returning[kind, j].start()
+            else:
+                stores[4 * kind].start()
 
     add_up(1)
     stats = join(1, stats)
@@ -331,7 +347,6 @@
     stores[2].start()
     stores[3].start()
     add_up(0)
-    stores[0].start()
 
     teacher_copy.wait_send()
     for copy in telling:
@@ -379,29 +394,34 @@
         copy.start()
     for copy in small[:2]:
         copy.wait()
+
+    def share_out(inner_product):
+        inner_product = inner_product * table[3].astype(F32)
+        expert = row_experts(grp // 2)
+        for k in range(4):
+            pgr[k : k + 1, :] = jnp.sum(
+                jnp.where(ids[k : k + 1, :] == expert, inner_product, 0.0), axis=0, keepdims=True
+            )
+        store.start()
+
     inner_product = jnp.zeros((EXPERTS * CAP, 128), F32)
     row_stores = []
     for i, cut in enumerate(cuts):
         for copy in big[i]:
             copy.wait()
         rows = back[0, :, :, cut].reshape(EXPERTS * CAP, STEP)
+        inner_product = inner_product + dot_nt(rows, cot[:, cut])
+        if i == len(cuts) - 1:
+            share_out(inner_product)
         lay[:, cut] = (dot(table[0], rows) + dot(table[1], rows)).astype(BF16)
         ing[:, cut] = dot(table[2], back[1, :, :, cut].reshape(EXPERTS * CAP, STEP)).astype(BF16)
         for j, (src, dst) in enumerate(((lay, lay_h), (ing, ing_h))):
             copy = pltpu.make_async_copy(src.at[:, cut], dst.at[:, cut], row_sem.at[j, i])
             copy.start()
             row_stores.append(copy)
-        inner_product = inner_product + dot_nt(rows, cot[:, cut])
     for arrived, copy in zip(small[2:], handed):
         arrived.wait()
         copy.start()
-    inner_product = inner_product * table[3].astype(F32)
-    expert = row_experts(grp // 2)
-    for k in range(4):
-        pgr[k : k + 1, :] = jnp.sum(
-            jnp.where(ids[k : k + 1, :] == expert, inner_product, 0.0), axis=0, keepdims=True
-        )
-    store.start()
     for copy in handed + row_stores + [store]:
         copy.wait()
 
@@ -451,7 +471,7 @@
             pltpu.VMEM((2,) + w_gate.shape[1:], BF16),
             pltpu.VMEM(w_down.shape[1:], BF16),
             dma((9,)),
-            dma((4,)),
+            dma((5,)),
             dma((3,)),
             dma((3,)),
             dma((2, 8)),

time: 67.1 us -> 67.1 us (level)
  no operation moved by 1% of the time
where the time goes in v4:
time: 67.1 us; the launch traced here: 66.9 us
  Pallas kernels  66.3 us (99%)
    pallas_call x1, Pallas kernels, body(): pl.pallas_call(expert_kernel, name='experts', out_shape=(jax.ShapeDtypeSt...  62.9 us
    pallas_call x1, Pallas kernels, body(): pl.pallas_call(token_kernel, name='tokens', out_shape=(jax.ShapeDtypeStru...  3.31 us

profile of v4, /device:TPU:2, one launch (start us, length us, event | category | flops | bytes accessed | tf_op | source)
XLA Modules:
  0.0 66.9 jit_solution(1344140911295030926)
XLA Ops:
  0.6 62.9 %experts.1 = (bf16[2,4,32,2048]{3,2,1,0:T(8,128)(2,1)}, bf16[4,128,128]{2,1,0:T(8,128)(2,1)}, f32[1,8]{1,0:T(1,128)}, bf16[1,8,9496]{2,1,0:T(8,128)(2,1)}) custom-call(bf16[128,2048]{1,0:T(8,128)(2,1)} %tok_h.1, bf16[128,2048]{1,0:T(8,128)(2,1)} %cot_h.3, s32[4,128]{1,0:T(4,128)} %bitcast.7, f32[4,128]{1,0:T(4,128)} %bitcast.9, ...), custom_call_target="tpu_custom_call" | custom-call | tf_op jit(solution)/shard_map/experts/pallas_call | solution.py:438
  63.6 3.3 %tokens.1 = (bf16[128,2048]{1,0:T(8,128)(2,1)}, bf16[128,2048]{1,0:T(8,128)(2,1)}, f32[4,128]{1,0:T(4,128)}, f32[1,8]{1,0:T(1,128)}, bf16[1,8,9496]{2,1,0:T(8,128)(2,1)}) custom-call(bf16[128,2048]{1,0:T(8,128)(2,1)} %cot_h.3, s32[4,128]{1,0:T(4,128)} %bitcast.8, bf16[2,4,32,2048]{3,2,1,0:T(8,128)(2,1)} %get-tuple-element.14.back_h, ...), custom_call_target="tpu_custom_call" | custom-call | tf_op jit(solution)/shard_map/tokens/pallas_call | solution.py:492
